TPU v7x, 128 devices: a whole 4x4x4 slice. The times are simulated.
128 devices in a mesh: dp: 128 (over y, z, x, core).
Axes of the slice: x: 4, y: 4, z: 4, core: 2. Of those that a mesh axis runs over, the one named last changes fastest.
Arguments:
- images: bfloat16 [32768, 1152], P('dp'), may hold values from -0.7 to 0.7
- texts: bfloat16 [32768, 1152], P('dp'), may hold values from -0.9 to 0.9
- partner: int32 [3, 128], replicated, may hold values from 0 to 127, as said below
- logit_scale: float32 [1], replicated, may hold values from 4 to 16
- logit_bias: float32 [1], replicated, may hold values from -3 to -1
Outputs:
- image_grad: float32 [32768, 1152], P('dp')
- text_grad: float32 [32768, 1152], P('dp')
- row_loss: float32 [32768], P('dp')
Inputs may be any that keep to these rules, and one draw needn't show every extreme that they name: partner[r, d] = d XOR m_r, with m_r of 1 to 127 for round r, the 3 numbers distinct.
All inputs are finite; a program needn't handle non-finite values.
Results may differ from a plain program's by a relative error of at most 0.0023.
Values may be sent and summed in bfloat16 or wider, within the bound.
No kernel may reach another device: no remote copies, remote signals or barrier semaphores. Data moves between devices by JAX's collectives and lax.ppermute only.
A program may use at most 64 MiB of HBM per device.

v0:
```python
import functools

import jax
import jax.numpy as jnp
from jax import lax
from jax.experimental import pallas as pl
from jax.experimental.pallas import tpu as pltpu
from jax.sharding import PartitionSpec as P

ROUNDS = 3
NORM_EPS = 1e-06
PIECE = 8
VMEM_BYTES = 48 * 1024 * 1024
NT = (((1,), (1,)), ((), ()))


def inverse_length(values):
    return lax.rsqrt(jnp.sum(values * values, axis=-1, keepdims=True) + NORM_EPS)


def halve_kernel(images_ref, texts_ref, half_ref):
    for slot, source in enumerate((images_ref, texts_ref)):
        values = source[...].astype(jnp.float32)
        half_ref[slot] = (values * inverse_length(values)).astype(jnp.bfloat16)


def halve(images, texts):
    rows, width = images.shape
    step = rows // 4
    return pl.pallas_call(
        halve_kernel,
        grid=(rows // step,),
        in_specs=[pl.BlockSpec((step, width), lambda i: (i, 0))] * 2,
        out_specs=pl.BlockSpec((2, step, width), lambda i: (0, i, 0)),
        out_shape=jax.ShapeDtypeStruct((2, rows, width), jnp.bfloat16),
        compiler_params=pltpu.CompilerParams(vmem_limit_bytes=VMEM_BYTES),
    )(images, texts)


def own_kernel(scalars_ref, half_ref, img_sum_ref, txt_sum_ref, row_ref):
    scale, bias = scalars_ref[0], scalars_ref[1]
    img, txt = half_ref[0], half_ref[1]
    rows = img.shape[0]
    diagonal = lax.broadcasted_iota(jnp.int32, (rows, rows), 0) == lax.broadcasted_iota(
        jnp.int32, (rows, rows), 1
    )
    logits = scale * lax.dot_general(img, txt, NT, preferred_element_type=jnp.float32) + bias
    signed = jnp.where(diagonal, -logits, logits)
    row_ref[...] = jnp.sum(softplus(signed), axis=-1, keepdims=True)
    positive = jnp.where(diagonal, 1.0, 0.0)
    weights = (sigmoid(logits) - positive).astype(jnp.bfloat16)
    img_sum_ref[...] = scale * jnp.dot(weights, txt, preferred_element_type=jnp.float32)
    turned = scale * lax.dot_general(txt, img, NT, preferred_element_type=jnp.float32) + bias
    weights = (sigmoid(turned) - positive).astype(jnp.bfloat16)
    txt_sum_ref[...] = scale * jnp.dot(weights, img, preferred_element_type=jnp.float32)


def softplus(x):
    return jnp.maximum(x, 0.0) + jnp.log1p(jnp.exp(-jnp.abs(x)))


def sigmoid(x):
    return 1.0 / (1.0 + jnp.exp(-x))


def own_terms(scalars, half):
    _, rows, width = half.shape
    return pl.pallas_call(
        own_kernel,
        in_specs=[
            pl.BlockSpec(memory_space=pltpu.SMEM),
            pl.BlockSpec(memory_space=pltpu.VMEM),
        ],
        out_specs=[pl.BlockSpec(memory_space=pltpu.VMEM)] * 3,
        out_shape=[
            jax.ShapeDtypeStruct((rows, width), jnp.float32),
            jax.ShapeDtypeStruct((rows, width), jnp.float32),
            jax.ShapeDtypeStruct((rows, 1), jnp.float32),
        ],
        compiler_params=pltpu.CompilerParams(vmem_limit_bytes=VMEM_BYTES),
        cost_estimate=pl.CostEstimate(
            flops=8 * rows * rows * width, bytes_accessed=12 * rows * width, transcendentals=4 * rows * rows
        ),
    )(scalars, half)


def route_kernel(flips_ref, same_ref, other_ref, out_ref):
    chips = same_ref.shape[0]
    for r in range(ROUNDS):
        chip_flip = flips_ref[r] // 2
        core_flip = flips_ref[r] % 2
        for core, source in enumerate((same_ref, other_ref)):

            @pl.when(core_flip == core)
            def _():
                def copy(t, carry):
                    out_ref[t, r] = source[lax.bitwise_xor(t, chip_flip)]
                    return carry

                lax.fori_loop(0, chips, copy, 0, unroll=8)


def route(flips, same, other):
    chips, piece, width = same.shape
    return pl.pallas_call(
        route_kernel,
        in_specs=[pl.BlockSpec(memory_space=pltpu.SMEM)]
        + [pl.BlockSpec(memory_space=pltpu.VMEM)] * 2,
        out_specs=pl.BlockSpec(memory_space=pltpu.VMEM),
        out_shape=jax.ShapeDtypeStruct((chips, ROUNDS, piece, width), same.dtype),
        compiler_params=pltpu.CompilerParams(vmem_limit_bytes=VMEM_BYTES),
    )(flips, same, other)


def finish(values, summed):
    inverse = inverse_length(values)
    unit = values * inverse
    radial = jnp.sum(unit * summed, axis=-1, keepdims=True)
    return (summed - unit * radial) * inverse


def rounds_kernel(
    scalars_ref, images_ref, texts_ref, half_ref, far_ref, img_sum_ref, txt_sum_ref, row_ref,
    image_grad_ref, text_grad_ref, loss_ref,
):
    scale, bias = scalars_ref[0], scalars_ref[1]
    img, txt = half_ref[0], half_ref[1]
    rows, width = img.shape
    pieces = far_ref.shape[0] // 2
    row_total = row_ref[...]
    img_sum = img_sum_ref[...]
    txt_sum = txt_sum_ref[...]
    for r in range(ROUNDS):
        far_img = far_ref[:pieces, r].reshape(rows, width)
        far_txt = far_ref[pieces:, r].reshape(rows, width)
        logits = scale * lax.dot_general(img, far_txt, NT, preferred_element_type=jnp.float32) + bias
        row_total = row_total + jnp.sum(softplus(logits), axis=-1, keepdims=True)
        weights = sigmoid(logits).astype(jnp.bfloat16)
        img_sum = img_sum + scale * jnp.dot(weights, far_txt, preferred_element_type=jnp.float32)
        turned = scale * lax.dot_general(txt, far_img, NT, preferred_element_type=jnp.float32) + bias
        weights = sigmoid(turned).astype(jnp.bfloat16)
        term = scale * jnp.dot(weights, far_img, preferred_element_type=jnp.float32)
        txt_sum = txt_sum + term.astype(jnp.bfloat16).astype(jnp.float32)
    image_grad_ref[...] = finish(images_ref[...].astype(jnp.float32), img_sum)
    text_grad_ref[...] = finish(texts_ref[...].astype(jnp.float32), txt_sum)
    loss_ref[...] = row_total * (1.0 / ((ROUNDS + 1) * rows))


def all_rounds(scalars, images, texts, half, far, img_sum, txt_sum, row_total):
    rows, width = images.shape
    return pl.pallas_call(
        rounds_kernel,
        in_specs=[pl.BlockSpec(memory_space=pltpu.SMEM)]
        + [pl.BlockSpec(memory_space=pltpu.VMEM)] * 7,
        out_specs=[pl.BlockSpec(memory_space=pltpu.VMEM)] * 3,
        out_shape=[
            jax.ShapeDtypeStruct((rows, width), jnp.float32),
            jax.ShapeDtypeStruct((rows, width), jnp.float32),
            jax.ShapeDtypeStruct((rows, 1), jnp.float32),
        ],
        compiler_params=pltpu.CompilerParams(vmem_limit_bytes=VMEM_BYTES),
    )(scalars, images, texts, half, far, img_sum, txt_sum, row_total)


def body(num_dev, images, texts, partner, logit_scale, logit_bias):
    rows, width = images.shape
    chips = num_dev // 2
    same_core = [[2 * chip + core for chip in range(chips)] for core in range(2)]
    exchange = functools.partial(
        lax.all_to_all, axis_name="dp", split_axis=0, concat_axis=0, tiled=True, axis_index_groups=same_core
    )
    scalars = jnp.concatenate([logit_scale, logit_bias])
    flips = partner[:, 0]
    half = halve(images, texts)
    spread = exchange(half.reshape(chips, PIECE, width))
    img_sum, txt_sum, row_total = own_terms(scalars, half)
    sibling = lax.ppermute(spread, "dp", [(i, i ^ 1) for i in range(num_dev)])
    far = exchange(route(flips, spread, sibling))
    image_grad, text_grad, loss = all_rounds(
        scalars, images, texts, half, far, img_sum, txt_sum, row_total
    )
    return image_grad, text_grad, loss.reshape(rows)


def solution(mesh):
    return jax.shard_map(
        functools.partial(body, mesh.devices.size),
        mesh=mesh,
        in_specs=(P("dp", None), P("dp", None), P(), P(), P()),
        out_specs=(P("dp", None), P("dp", None), P("dp")),
        check_vma=False,
    )
```

profile of v0, /device:TPU:0, one launch (start us, length us, event | category | flops | bytes accessed | tf_op | source)
XLA Modules:
  0.0 105.4 jit_solution(3676275695765581505)
XLA Ops:
  0.6 0.0 copy-start
  0.6 1.1 %copy-done = bf16[256,1152]{1,0:T(8,128)(2,1)S(1)} copy-done((bf16[256,1152]{1,0:T(8,128)(2,1)S(1)}, bf16[256,1152]{1,0:T(8,128)(2,1)}, u32[]{:S(2)}) %copy-start) | copy-done | bytes 589848
  1.7 1.1 %copy-done.2 = bf16[256,1152]{1,0:T(8,128)(2,1)S(1)} copy-done((bf16[256,1152]{1,0:T(8,128)(2,1)S(1)}, bf16[256,1152]{1,0:T(8,128)(2,1)}, u32[]{:S(2)}) %copy-start.2) | copy-done | bytes 589848
  2.8 0.7 shard_map.76.half_ref
  3.5 0.0 copy-start.9
  3.5 31.6 %all_to_all.10.same_ref = bf16[64,8,1152]{2,1,0:T(8,128)(2,1)S(1)} all-to-all(bf16[64,8,1152]{2,1,0:T(8,128)(2,1)S(1)} %bitcast.1), channel_id=1, replica_groups={{0,2,4,6,8,10,12,14,16,18,20,22,24,26,28,30,32,34,36,38,40,42,44,46,48,..., dimensions={0} | all-to-all | bytes 2359296 | tf_op jit(solution)/shard_map/all_to_all | solution.py:175
  35.1 0.0 collective-permute-start
  35.1 0.1 slice_reduce_fusion.flips_ref
  35.2 2.7 %collective-permute-done.other_ref = bf16[64,8,1152]{2,1,0:T(8,128)(2,1)S(1)} collective-permute-done((bf16[64,8,1152]{2,1,0:T(8,128)(2,1)S(1)}, bf16[64,8,1152]{2,1,0:T(8,128)(2,1)S(1)}, u32[]{:S(2)}, u32[]{:S(2)}) %collective-permute-start) | collective-permute-done | bytes 1179680 | tf_op jit(solution)/shard_map/ppermute | solution.py:177
  38.0 2.7 %shard_map.77 = bf16[64,3,8,1152]{3,2,1,0:T(8,128)(2,1)} custom-call(s32[3]{0:T(128)S(1)} %slice_reduce_fusion.flips_ref, bf16[64,8,1152]{2,1,0:T(8,128)(2,1)S(1)} %all_to_all.10.same_ref, bf16[64,8,1152]{2,1,0:T(8,128)(2,1)S(1)} %collective-permute-done.other_ref), custom_call_target="tpu_custom_call" | custom-call | tf_op jit(solution)/shard_map/pallas_call | solution.py:105
  40.7 5.6 %all-to-all-start.1 = ((bf16[64,3,8,1152]{3,2,1,0:T(8,128)(2,1)}), bf16[64,3,8,1152]{3,2,1,0:T(8,128)(2,1)}, u32[]{:S(2)}, u32[]{:S(2)}) async-start(bf16[64,3,8,1152]{3,2,1,0:T(8,128)(2,1)} %shard_map.77), calls=%async_computation.1 | async-start | bytes 7077888 | tf_op jit(solution)/shard_map/all_to_all | solution.py:178
  46.3 0.0 copy-start.1
  46.3 0.0 copy-start.3
  47.7 0.1 pad_maximum_fusion.scalars_ref
  47.8 2.3 %shard_map.78 = (f32[256,1152]{1,0:T(8,128)S(1)}, f32[256,1152]{1,0:T(8,128)S(1)}, f32[256,1]{1,0:T(8,128)S(1)}) custom-call(f32[2]{0:T(128)S(1)} %pad_maximum_fusion.scalars_ref, bf16[2,256,1152]{2,1,0:T(8,128)(2,1)S(1)} %shard_map.76.half_ref), custom_call_target="tpu_custom_call" | custom-call | flops 603979776 | bytes 3538944 | tf_op jit(solution)/shard_map/pallas_call | solution.py:68
  50.1 0.0 copy-start.4
  50.1 1.0 copy-done.4
  51.1 0.7 copy-done.6
  51.8 42.3 %all-to-all-done.1.far_ref = bf16[64,3,8,1152]{3,2,1,0:T(8,128)(2,1)} async-done(((bf16[64,3,8,1152]{3,2,1,0:T(8,128)(2,1)}), bf16[64,3,8,1152]{3,2,1,0:T(8,128)(2,1)}, u32[]{:S(2)}, u32[]{:S(2)}) %all-to-all-start.1) | async-done | bytes 3538976 | tf_op jit(solution)/shard_map/all_to_all | solution.py:178
  94.1 1.3 %copy-done.5 = f32[256,1152]{1,0:T(8,128)S(1)} copy-done((f32[256,1152]{1,0:T(8,128)S(1)}, f32[256,1152]{1,0:T(8,128)}, u32[]{:S(2)}) %copy-start.5) | copy-done | bytes 1179672
  95.3 0.9 copy-done.7
  96.2 6.9 %shard_map.79 = (f32[256,1152]{1,0:T(8,128)}, f32[256,1152]{1,0:T(8,128)}, f32[256,1]{1,0:T(8,128)S(1)}) custom-call(f32[2]{0:T(128)S(1)} %pad_maximum_fusion.scalars_ref, bf16[256,1152]{1,0:T(8,128)(2,1)S(1)} %copy-done.1, bf16[256,1152]{1,0:T(8,128)(2,1)S(1)} %copy-done.3, bf16[2,256,1152]{2,1,0:T(8,128)(2,1)S(1)} %shard_map.76.half_ref, ...), custom_call_target="tpu_custom_call" | custom-call | tf_op jit(solution)/shard_map/pallas_call | solution.py:151
  103.2 0.6 copy-done.8
  103.8 1.6 %reduce.1 = f32[256]{0:T(256)} reduce(f32[256,1]{1,0:T(8,128)} %copy-done.8, f32[]{:T(128)} %constant.1), dimensions={1}, to_apply=%get-tuple-element.14.reduce_sub_computation | reduce | bytes 2052 | tf_op jit(solution)/shard_map/pallas_call | solution.py:151
  (8 shorter events, 0.0 us)
Async XLA Ops:
  0.6 1.1 %copy-start = (bf16[256,1152]{1,0:T(8,128)(2,1)S(1)}, bf16[256,1152]{1,0:T(8,128)(2,1)}, u32[]{:S(2)}) copy-start(bf16[256,1152]{1,0:T(8,128)(2,1)} %images_ref.3) | copy-start | bytes 1769476
  1.7 1.1 %copy-start.2 = (bf16[256,1152]{1,0:T(8,128)(2,1)S(1)}, bf16[256,1152]{1,0:T(8,128)(2,1)}, u32[]{:S(2)}) copy-start(bf16[256,1152]{1,0:T(8,128)(2,1)} %texts_ref.3) | copy-start | bytes 1769476
  3.5 31.6 %copy-start.9 = (s32[3,128]{1,0:T(4,128)S(1)}, s32[3,128]{1,0:T(4,128)}, u32[]{:S(2)}) copy-start(s32[3,128]{1,0:T(4,128)} %param.7) | copy-start | bytes 4612
  35.1 2.8 %collective-permute-start = (bf16[64,8,1152]{2,1,0:T(8,128)(2,1)S(1)}, bf16[64,8,1152]{2,1,0:T(8,128)(2,1)S(1)}, u32[]{:S(2)}, u32[]{:S(2)}) collective-permute-start(bf16[64,8,1152]{2,1,0:T(8,128)(2,1)S(1)} %all_to_all.10.same_ref), channel_id=1, source_target_pairs={{0,1},{1,0},{2,3},{3,2},{4,5},{5,4},{6,7},{7,6},{8,9},{9,8},{10,11... | collective-permute-start | bytes 3538952 | tf_op jit(solution)/shard_map/ppermute | solution.py:177
  40.7 53.4 %all-to-all-start.1 = ((bf16[64,3,8,1152]{3,2,1,0:T(8,128)(2,1)}), bf16[64,3,8,1152]{3,2,1,0:T(8,128)(2,1)}, u32[]{:S(2)}, u32[]{:S(2)}) async-start(bf16[64,3,8,1152]{3,2,1,0:T(8,128)(2,1)} %shard_map.77), calls=%async_computation.1 | async-start | bytes 7077888 | tf_op jit(solution)/shard_map/all_to_all | solution.py:178
  46.3 47.8 %copy-start.1 = (bf16[256,1152]{1,0:T(8,128)(2,1)S(1)}, bf16[256,1152]{1,0:T(8,128)(2,1)}, u32[]{:S(2)}) copy-start(bf16[256,1152]{1,0:T(8,128)(2,1)} %images_ref.3) | copy-start | bytes 1769476
  46.3 47.7 %copy-start.3 = (bf16[256,1152]{1,0:T(8,128)(2,1)S(1)}, bf16[256,1152]{1,0:T(8,128)(2,1)}, u32[]{:S(2)}) copy-start(bf16[256,1152]{1,0:T(8,128)(2,1)} %texts_ref.3) | copy-start | bytes 1769476
  50.1 1.0 copy-start.4
  51.1 0.7 copy-start.6
  94.1 1.3 %copy-start.5 = (f32[256,1152]{1,0:T(8,128)S(1)}, f32[256,1152]{1,0:T(8,128)}, u32[]{:S(2)}) copy-start(f32[256,1152]{1,0:T(8,128)} %copy-done.4) | copy-start | bytes 3538948
  95.3 0.9 copy-start.7
  103.2 0.6 copy-start.8
where the time goes:
time: 106 us; the launch traced here: 105 us
  waiting for transfers between devices  45 us (42%)
  blocking collectives  31.6 us (30%)
  Pallas kernels  12.7 us (12%)
  local copies, waits for them, and re-layouts  6.74 us (6%)
  starting transfers between devices  5.6 us (5%)
  between operations  2.09 us (2%)
  other arithmetic  1.66 us (2%)
    all_to_all x1, waiting for transfers between devices, body(): far = exchange(route(flips, spread, sibling))  42.3 us
    all_to_all x1, blocking collectives, body(): spread = exchange(half.reshape(chips, PIECE, width))  31.6 us
    pallas_call x1, Pallas kernels, all_rounds(): pl.pallas_call(rounds_kernel, in_specs=[pl.BlockSpec(memory_space=pltpu.S...  6.93 us
    unnamed x20, local copies, waits for them, and re-layouts  6.62 us
    all_to_all x1, starting transfers between devices, body(): far = exchange(route(flips, spread, sibling))  5.6 us
    pallas_call x1, Pallas kernels, route(): pl.pallas_call(route_kernel, in_specs=[pl.BlockSpec(memory_space=pltpu.SM...  2.73 us
    ppermute x1, waiting for transfers between devices, body(): sibling = lax.ppermute(spread, 'dp', [(i, i ^ 1) for i in range(num_dev)])  2.73 us
    pallas_call x1, Pallas kernels, own_terms(): pl.pallas_call(own_kernel, in_specs=[pl.BlockSpec(memory_space=pltpu.SMEM...  2.33 us
  transfers between devices with their start and end apart: 2, of which 2 were waited for; matrix products, arithmetic and copies ran while one was open for 0% of the time, Pallas kernels for 2%

commit v1 on v0

--- a/solution.py
+++ b/solution.py
@@ -10,7 +10,8 @@
 ROUNDS = 3
 NORM_EPS = 1e-06
 PIECE = 8
-VMEM_BYTES = 48 * 1024 * 1024
+VMEM_BYTES = 20 * 1024 * 1024
+FULL_VMEM_BYTES = 61 * 1024 * 1024
 NT = (((1,), (1,)), ((), ()))
 
 
@@ -26,18 +27,18 @@
 
 def halve(images, texts):
     rows, width = images.shape
-    step = rows // 4
+    step = rows // 2
     return pl.pallas_call(
         halve_kernel,
         grid=(rows // step,),
         in_specs=[pl.BlockSpec((step, width), lambda i: (i, 0))] * 2,
         out_specs=pl.BlockSpec((2, step, width), lambda i: (0, i, 0)),
         out_shape=jax.ShapeDtypeStruct((2, rows, width), jnp.bfloat16),
-        compiler_params=pltpu.CompilerParams(vmem_limit_bytes=VMEM_BYTES),
+        compiler_params=pltpu.CompilerParams(vmem_limit_bytes=FULL_VMEM_BYTES),
     )(images, texts)
 
 
-def own_kernel(scalars_ref, half_ref, img_sum_ref, txt_sum_ref, row_ref):
+def own_kernel(scalars_ref, half_ref, img_sum_ref, txt_sum_ref, loss_ref):
     scale, bias = scalars_ref[0], scalars_ref[1]
     img, txt = half_ref[0], half_ref[1]
     rows = img.shape[0]
@@ -46,7 +47,7 @@
     )
     logits = scale * lax.dot_general(img, txt, NT, preferred_element_type=jnp.float32) + bias
     signed = jnp.where(diagonal, -logits, logits)
-    row_ref[...] = jnp.sum(softplus(signed), axis=-1, keepdims=True)
+    loss_ref[...] = softplus(signed)
     positive = jnp.where(diagonal, 1.0, 0.0)
     weights = (sigmoid(logits) - positive).astype(jnp.bfloat16)
     img_sum_ref[...] = scale * jnp.dot(weights, txt, preferred_element_type=jnp.float32)
@@ -75,7 +76,7 @@
         out_shape=[
             jax.ShapeDtypeStruct((rows, width), jnp.float32),
             jax.ShapeDtypeStruct((rows, width), jnp.float32),
-            jax.ShapeDtypeStruct((rows, 1), jnp.float32),
+            jax.ShapeDtypeStruct((rows, rows), jnp.float32),
         ],
         compiler_params=pltpu.CompilerParams(vmem_limit_bytes=VMEM_BYTES),
         cost_estimate=pl.CostEstimate(
@@ -120,21 +121,21 @@
 
 
 def rounds_kernel(
-    scalars_ref, images_ref, texts_ref, half_ref, far_ref, img_sum_ref, txt_sum_ref, row_ref,
+    scalars_ref, images_ref, texts_ref, half_ref, far_ref, img_sum_ref, txt_sum_ref, own_loss_ref,
     image_grad_ref, text_grad_ref, loss_ref,
 ):
     scale, bias = scalars_ref[0], scalars_ref[1]
     img, txt = half_ref[0], half_ref[1]
     rows, width = img.shape
     pieces = far_ref.shape[0] // 2
-    row_total = row_ref[...]
+    losses = own_loss_ref[...]
     img_sum = img_sum_ref[...]
     txt_sum = txt_sum_ref[...]
     for r in range(ROUNDS):
         far_img = far_ref[:pieces, r].reshape(rows, width)
         far_txt = far_ref[pieces:, r].reshape(rows, width)
         logits = scale * lax.dot_general(img, far_txt, NT, preferred_element_type=jnp.float32) + bias
-        row_total = row_total + jnp.sum(softplus(logits), axis=-1, keepdims=True)
+        losses = losses + softplus(logits)
         weights = sigmoid(logits).astype(jnp.bfloat16)
         img_sum = img_sum + scale * jnp.dot(weights, far_txt, preferred_element_type=jnp.float32)
         turned = scale * lax.dot_general(txt, far_img, NT, preferred_element_type=jnp.float32) + bias
@@ -143,10 +144,10 @@
         txt_sum = txt_sum + term.astype(jnp.bfloat16).astype(jnp.float32)
     image_grad_ref[...] = finish(images_ref[...].astype(jnp.float32), img_sum)
     text_grad_ref[...] = finish(texts_ref[...].astype(jnp.float32), txt_sum)
-    loss_ref[...] = row_total * (1.0 / ((ROUNDS + 1) * rows))
+    loss_ref[...] = jnp.sum(losses.T, axis=0, keepdims=True) * (1.0 / ((ROUNDS + 1) * rows))
 
 
-def all_rounds(scalars, images, texts, half, far, img_sum, txt_sum, row_total):
+def all_rounds(scalars, images, texts, half, far, img_sum, txt_sum, losses):
     rows, width = images.shape
     return pl.pallas_call(
         rounds_kernel,
@@ -156,10 +157,10 @@
         out_shape=[
             jax.ShapeDtypeStruct((rows, width), jnp.float32),
             jax.ShapeDtypeStruct((rows, width), jnp.float32),
-            jax.ShapeDtypeStruct((rows, 1), jnp.float32),
+            jax.ShapeDtypeStruct((1, rows), jnp.float32),
         ],
         compiler_params=pltpu.CompilerParams(vmem_limit_bytes=VMEM_BYTES),
-    )(scalars, images, texts, half, far, img_sum, txt_sum, row_total)
+    )(scalars, images, texts, half, far, img_sum, txt_sum, losses)
 
 
 def body(num_dev, images, texts, partner, logit_scale, logit_bias):
@@ -173,11 +174,13 @@
     flips = partner[:, 0]
     half = halve(images, texts)
     spread = exchange(half.reshape(chips, PIECE, width))
-    img_sum, txt_sum, row_total = own_terms(scalars, half)
+    half, spread = lax.optimization_barrier((half, spread))
     sibling = lax.ppermute(spread, "dp", [(i, i ^ 1) for i in range(num_dev)])
+    img_sum, txt_sum, losses = own_terms(scalars, half)
+    sibling, img_sum = lax.optimization_barrier((sibling, img_sum))
     far = exchange(route(flips, spread, sibling))
     image_grad, text_grad, loss = all_rounds(
-        scalars, images, texts, half, far, img_sum, txt_sum, row_total
+        scalars, images, texts, half, far, img_sum, txt_sum, losses
     )
     return image_grad, text_grad, loss.reshape(rows)
 

time: 106 us -> 96.6 us (0.911)
  blocking collectives: 31.6 us -> 82.8 us
  waiting for transfers between devices: 45 us -> 0.01 us
  local copies, waits for them, and re-layouts: 6.74 us -> 0.13 us
  starting transfers between devices: 5.6 us -> 0.01 us
  other arithmetic: 1.66 us -> 0.08 us
  Pallas kernels: 12.7 us -> 11.3 us
    all_to_all x0 -> x1, blocking collectives: none -> 50.9 us  [body(): far = exchange(route(flips, spread, sibling))]
    all_to_all x1 -> x0, waiting for transfers between devices: 42.3 us -> none  [body(): far = exchange(route(flips, spread, sibling))]
    unnamed x20 -> x8, local copies, waits for them, and re-layouts: 6.62 us -> 0.02 us
    all_to_all x1 -> x0, starting transfers between devices: 5.6 us -> none  [body(): far = exchange(route(flips, spread, sibling))]
    ppermute x1, waiting for transfers between devices: 2.73 us -> 0.01 us  [body(): sibling = lax.ppermute(spread, 'dp', [(i, i ^ 1) for i in range(num_dev)])]
    pallas_call x1, Pallas kernels: 2.73 us -> 0.94 us  [route(): pl.pallas_call(route_kernel, in_specs=[pl.BlockSpec(memory_space=pltpu.SM...]
    pallas_call x1, Pallas kernels: 0.7 us -> 2.31 us  [halve(): pl.pallas_call(halve_kernel, grid=(rows // step,), in_specs=[pl.BlockSpec...]
    pallas_call x1 -> x0, other arithmetic: 1.58 us -> none  [all_rounds(): pl.pallas_call(rounds_kernel, in_specs=[pl.BlockSpec(memory_space=pltpu.S...]
  transfers between devices with their start and end apart: 2 -> 1, of which waited for: 2 -> 0; matrix products, arithmetic and copies ran while one was open for 0% -> 0% of each run, Pallas kernels for 2% -> 2%
where the time goes in v1:
time: 96.6 us; the launch traced here: 96.3 us
  blocking collectives  82.8 us (86%)
  Pallas kernels  11.3 us (12%)
  between operations  1.97 us (2%)
    all_to_all x1, blocking collectives, body(): far = exchange(route(flips, spread, sibling))  50.9 us
    all_to_all x1, blocking collectives, body(): spread = exchange(half.reshape(chips, PIECE, width))  31.9 us
    pallas_call x1, Pallas kernels, all_rounds(): pl.pallas_call(rounds_kernel, in_specs=[pl.BlockSpec(memory_space=pltpu.S...  5.72 us
    pallas_call x1, Pallas kernels, own_terms(): pl.pallas_call(own_kernel, in_specs=[pl.BlockSpec(memory_space=pltpu.SMEM...  2.34 us
    pallas_call x1, Pallas kernels, halve(): pl.pallas_call(halve_kernel, grid=(rows // step,), in_specs=[pl.BlockSpec...  2.31 us
  transfers between devices with their start and end apart: 1, of which 0 were waited for; matrix products, arithmetic and copies ran while one was open for 0% of the time, Pallas kernels for 2%

profile of v1, /device:TPU:0, one launch (start us, length us, event | category | flops | bytes accessed | tf_op | source)
XLA Modules:
  0.0 96.3 jit_solution(13254013841768706704)
XLA Ops:
  0.6 2.3 %shard_map.76.half_ref = bf16[2,256,1152]{2,1,0:T(8,128)(2,1)} custom-call(bf16[256,1152]{1,0:T(8,128)(2,1)} %images_ref.3, bf16[256,1152]{1,0:T(8,128)(2,1)} %texts_ref.3), custom_call_target="tpu_custom_call" | custom-call | tf_op jit(solution)/shard_map/pallas_call | solution.py:31
  2.9 0.0 copy-start.3
  2.9 0.0 copy-start
  2.9 31.9 %all_to_all.10.same_ref = bf16[64,8,1152]{2,1,0:T(8,128)(2,1)S(1)} all-to-all(bf16[64,8,1152]{2,1,0:T(8,128)(2,1)} %bitcast.2), channel_id=1, replica_groups={{0,2,4,6,8,10,12,14,16,18,20,22,24,26,28,30,32,34,36,38,40,42,44,46,48,..., dimensions={0} | all-to-all | bytes 2359296 | tf_op jit(solution)/shard_map/all_to_all | solution.py:176
  34.9 0.0 collective-permute-start
  36.2 0.1 pad_maximum_fusion.scalars_ref
  36.3 0.0 copy-done.3
  36.3 0.1 slice_reduce_fusion.flips_ref
  36.4 0.0 copy-done
  36.4 2.3 %shard_map.77 = (f32[256,1152]{1,0:T(8,128)S(1)}, f32[256,1152]{1,0:T(8,128)S(1)}, f32[256,256]{1,0:T(8,128)S(1)}) custom-call(f32[2]{0:T(128)S(1)} %pad_maximum_fusion.scalars_ref, bf16[2,256,1152]{2,1,0:T(8,128)(2,1)S(1)} %copy-done), custom_call_target="tpu_custom_call" | custom-call | flops 603979776 | bytes 3538944 | tf_op jit(solution)/shard_map/pallas_call | solution.py:69
  38.7 0.0 collective-permute-done.other_ref
  38.7 0.9 shard_map.78
  39.7 0.0 copy-start.1
  39.7 0.0 copy-start.2
  39.7 50.9 %all_to_all.11.far_ref = bf16[64,3,8,1152]{3,2,1,0:T(8,128)(2,1)S(1)} all-to-all(bf16[64,3,8,1152]{3,2,1,0:T(8,128)(2,1)S(1)} %shard_map.78), channel_id=1, replica_groups={{0,2,4,6,8,10,12,14,16,18,20,22,24,26,28,30,32,34,36,38,40,42,44,46,48,..., dimensions={0} | all-to-all | bytes 7077888 | tf_op jit(solution)/shard_map/all_to_all | solution.py:181
  90.6 0.0 copy-done.1
  90.6 0.0 copy-done.2
  90.6 5.7 %shard_map.79 = (f32[256,1152]{1,0:T(8,128)}, f32[256,1152]{1,0:T(8,128)}, f32[1,256]{1,0:T(1,128)}) custom-call(f32[2]{0:T(128)S(1)} %pad_maximum_fusion.scalars_ref, bf16[256,1152]{1,0:T(8,128)(2,1)S(1)} %copy-done.1, bf16[256,1152]{1,0:T(8,128)(2,1)S(1)} %copy-done.2, bf16[2,256,1152]{2,1,0:T(8,128)(2,1)S(1)} %copy-done, ...), custom_call_target="tpu_custom_call" | custom-call | tf_op jit(solution)/shard_map/pallas_call | solution.py:152
Async XLA Ops:
  2.9 33.3 %copy-start.3 = (s32[3,128]{1,0:T(4,128)S(1)}, s32[3,128]{1,0:T(4,128)}, u32[]{:S(2)}) copy-start(s32[3,128]{1,0:T(4,128)} %param.7) | copy-start | bytes 4612
  2.9 33.5 %copy-start = (bf16[2,256,1152]{2,1,0:T(8,128)(2,1)S(1)}, bf16[2,256,1152]{2,1,0:T(8,128)(2,1)}, u32[]{:S(2)}) copy-start(bf16[2,256,1152]{2,1,0:T(8,128)(2,1)} %shard_map.76.half_ref) | copy-start | bytes 3538948
  34.9 3.9 %collective-permute-start = (bf16[64,8,1152]{2,1,0:T(8,128)(2,1)S(1)}, bf16[64,8,1152]{2,1,0:T(8,128)(2,1)S(1)}, u32[]{:S(2)}, u32[]{:S(2)}) collective-permute-start(bf16[64,8,1152]{2,1,0:T(8,128)(2,1)S(1)} %all_to_all.10.same_ref), channel_id=1, source_target_pairs={{0,1},{1,0},{2,3},{3,2},{4,5},{5,4},{6,7},{7,6},{8,9},{9,8},{10,11... | collective-permute-start | bytes 3538952 | tf_op jit(solution)/shard_map/ppermute | solution.py:178
  39.7 50.9 %copy-start.1 = (bf16[256,1152]{1,0:T(8,128)(2,1)S(1)}, bf16[256,1152]{1,0:T(8,128)(2,1)}, u32[]{:S(2)}) copy-start(bf16[256,1152]{1,0:T(8,128)(2,1)} %images_ref.3) | copy-start | bytes 1769476
  39.7 50.9 %copy-start.2 = (bf16[256,1152]{1,0:T(8,128)(2,1)S(1)}, bf16[256,1152]{1,0:T(8,128)(2,1)}, u32[]{:S(2)}) copy-start(bf16[256,1152]{1,0:T(8,128)(2,1)} %texts_ref.3) | copy-start | bytes 1769476

commit v2 on v1

--- a/solution.py
+++ b/solution.py
@@ -10,6 +10,7 @@
 ROUNDS = 3
 NORM_EPS = 1e-06
 PIECE = 8
+CHUNKS = 2
 VMEM_BYTES = 20 * 1024 * 1024
 FULL_VMEM_BYTES = 61 * 1024 * 1024
 NT = (((1,), (1,)), ((), ()))
@@ -122,29 +123,47 @@
 
 def rounds_kernel(
     scalars_ref, images_ref, texts_ref, half_ref, far_ref, img_sum_ref, txt_sum_ref, own_loss_ref,
-    image_grad_ref, text_grad_ref, loss_ref,
+    image_grad_ref, text_grad_ref, loss_ref, grads, loss, sems, loss_sem,
 ):
     scale, bias = scalars_ref[0], scalars_ref[1]
     img, txt = half_ref[0], half_ref[1]
     rows, width = img.shape
     pieces = far_ref.shape[0] // 2
+    step = rows // CHUNKS
+    copies = []
+
+    def send(slot, source, summed, out_ref):
+        for chunk in range(CHUNKS):
+            part = pl.ds(chunk * step, step)
+            grads[slot, part] = finish(
+                source[part].astype(jnp.float32), summed[chunk * step : (chunk + 1) * step]
+            )
+            copy = pltpu.make_async_copy(grads.at[slot, part], out_ref.at[part], sems.at[slot, chunk])
+            copy.start()
+            copies.append(copy)
+
+    far_txt = far_ref[pieces:].reshape(ROUNDS * rows, width)
+    logits = scale * lax.dot_general(img, far_txt, NT, preferred_element_type=jnp.float32) + bias
+    weights = sigmoid(logits).astype(jnp.bfloat16)
+    summed = img_sum_ref[...] + scale * jnp.dot(weights, far_txt, preferred_element_type=jnp.float32)
+    send(0, images_ref, summed, image_grad_ref)
+    parts = softplus(logits)
     losses = own_loss_ref[...]
-    img_sum = img_sum_ref[...]
-    txt_sum = txt_sum_ref[...]
+    for r in range(ROUNDS):
+        losses = losses + parts[:, r * rows : (r + 1) * rows]
+    loss[...] = jnp.sum(losses.T, axis=0, keepdims=True) * (1.0 / ((ROUNDS + 1) * rows))
+    copies.append(pltpu.make_async_copy(loss, loss_ref, loss_sem))
+    copies[-1].start()
+    summed = txt_sum_ref[...]
     for r in range(ROUNDS):
         far_img = far_ref[:pieces, r].reshape(rows, width)
-        far_txt = far_ref[pieces:, r].reshape(rows, width)
-        logits = scale * lax.dot_general(img, far_txt, NT, preferred_element_type=jnp.float32) + bias
-        losses = losses + softplus(logits)
+        logits = scale * lax.dot_general(txt, far_img, NT, preferred_element_type=jnp.float32) + bias
         weights = sigmoid(logits).astype(jnp.bfloat16)
-        img_sum = img_sum + scale * jnp.dot(weights, far_txt, preferred_element_type=jnp.float32)
-        turned = scale * lax.dot_general(txt, far_img, NT, preferred_element_type=jnp.float32) + bias
-        weights = sigmoid(turned).astype(jnp.bfloat16)
         term = scale * jnp.dot(weights, far_img, preferred_element_type=jnp.float32)
-        txt_sum = txt_sum + term.astype(jnp.bfloat16).astype(jnp.float32)
-    image_grad_ref[...] = finish(images_ref[...].astype(jnp.float32), img_sum)
-    text_grad_ref[...] = finish(texts_ref[...].astype(jnp.float32), txt_sum)
-    loss_ref[...] = jnp.sum(losses.T, axis=0, keepdims=True) * (1.0 / ((ROUNDS + 1) * rows))
+        summed = summed + term.astype(jnp.bfloat16).astype(jnp.float32)
+    send(1, texts_ref, summed, text_grad_ref)
+    for copy in copies:
+        copy.wait()
 
 
 def all_rounds(scalars, images, texts, half, far, img_sum, txt_sum, losses):
@@ -153,11 +172,17 @@
         rounds_kernel,
         in_specs=[pl.BlockSpec(memory_space=pltpu.SMEM)]
         + [pl.BlockSpec(memory_space=pltpu.VMEM)] * 7,
-        out_specs=[pl.BlockSpec(memory_space=pltpu.VMEM)] * 3,
+        out_specs=[pl.BlockSpec(memory_space=pltpu.HBM)] * 3,
         out_shape=[
             jax.ShapeDtypeStruct((rows, width), jnp.float32),
             jax.ShapeDtypeStruct((rows, width), jnp.float32),
             jax.ShapeDtypeStruct((1, rows), jnp.float32),
+        ],
+        scratch_shapes=[
+            pltpu.VMEM((2, rows, width), jnp.float32),
+            pltpu.VMEM((1, rows), jnp.float32),
+            pltpu.SemaphoreType.DMA((2, CHUNKS)),
+            pltpu.SemaphoreType.DMA,
         ],
         compiler_params=pltpu.CompilerParams(vmem_limit_bytes=VMEM_BYTES),
     )(scalars, images, texts, half, far, img_sum, txt_sum, losses)
@@ -174,10 +199,9 @@
     flips = partner[:, 0]
     half = halve(images, texts)
     spread = exchange(half.reshape(chips, PIECE, width))
-    half, spread = lax.optimization_barrier((half, spread))
+    img_sum, txt_sum, losses = own_terms(scalars, half)
+    spread, img_sum = lax.optimization_barrier((spread, img_sum))
     sibling = lax.ppermute(spread, "dp", [(i, i ^ 1) for i in range(num_dev)])
-    img_sum, txt_sum, losses = own_terms(scalars, half)
-    sibling, img_sum = lax.optimization_barrier((sibling, img_sum))
     far = exchange(route(flips, spread, sibling))
     image_grad, text_grad, loss = all_rounds(
         scalars, images, texts, half, far, img_sum, txt_sum, losses

time: 96.6 us -> 94.4 us (0.977)
  blocking collectives: 82.8 us -> 50.4 us
  waiting for transfers between devices: 0.01 us -> 17.6 us
  starting transfers between devices: 0.01 us -> 11.6 us
  local copies, waits for them, and re-layouts: 0.13 us -> 1.87 us
    all_to_all x1 -> x0, blocking collectives: 31.9 us -> none  [body(): spread = exchange(half.reshape(chips, PIECE, width))]
    all_to_all x0 -> x1, waiting for transfers between devices: none -> 14.9 us  [body(): spread = exchange(half.reshape(chips, PIECE, width))]
    all_to_all x0 -> x1, starting transfers between devices: none -> 11.6 us  [body(): spread = exchange(half.reshape(chips, PIECE, width))]
    ppermute x1, waiting for transfers between devices: 0.01 us -> 2.73 us  [body(): sibling = lax.ppermute(spread, 'dp', [(i, i ^ 1) for i in range(num_dev)])]
    unnamed x8 -> x16, local copies, waits for them, and re-layouts: 0.02 us -> 1.75 us
  transfers between devices with their start and end apart: 1 -> 2, of which waited for: 0 -> 2; matrix products, arithmetic and copies ran while one was open for 0% -> 0% of each run, Pallas kernels for 2% -> 2%
where the time goes in v2:
time: 94.4 us; the launch traced here: 94.1 us
  blocking collectives  50.4 us (53%)
  waiting for transfers between devices  17.6 us (19%)
  starting transfers between devices  11.6 us (12%)
  Pallas kernels  10.5 us (11%)
  between operations  2.02 us (2%)
  local copies, waits for them, and re-layouts  1.87 us (2%)
    all_to_all x1, blocking collectives, body(): far = exchange(route(flips, spread, sibling))  50.4 us
    all_to_all x1, waiting for transfers between devices, body(): spread = exchange(half.reshape(chips, PIECE, width))  14.9 us
    all_to_all x1, starting transfers between devices, body(): spread = exchange(half.reshape(chips, PIECE, width))  11.6 us
    pallas_call x1, Pallas kernels, all_rounds(): pl.pallas_call(rounds_kernel, in_specs=[pl.BlockSpec(memory_space=pltpu.S...  4.94 us
    ppermute x1, waiting for transfers between devices, body(): sibling = lax.ppermute(spread, 'dp', [(i, i ^ 1) for i in range(num_dev)])  2.73 us
    pallas_call x1, Pallas kernels, own_terms(): pl.pallas_call(own_kernel, in_specs=[pl.BlockSpec(memory_space=pltpu.SMEM...  2.34 us
    pallas_call x1, Pallas kernels, halve(): pl.pallas_call(halve_kernel, grid=(rows // step,), in_specs=[pl.BlockSpec...  2.31 us
  transfers between devices with their start and end apart: 2, of which 2 were waited for; matrix products, arithmetic and copies ran while one was open for 0% of the time, Pallas kernels for 2%

profile of v2, /device:TPU:0, one launch (start us, length us, event | category | flops | bytes accessed | tf_op | source)
XLA Modules:
  0.0 94.1 jit_solution(4010825531378027984)
XLA Ops:
  0.6 2.3 %shard_map.76.half_ref = bf16[2,256,1152]{2,1,0:T(8,128)(2,1)} custom-call(bf16[256,1152]{1,0:T(8,128)(2,1)} %images_ref.3, bf16[256,1152]{1,0:T(8,128)(2,1)} %texts_ref.3), custom_call_target="tpu_custom_call" | custom-call | tf_op jit(solution)/shard_map/pallas_call | solution.py:32
  2.9 11.6 %all-to-all-start = ((bf16[64,8,1152]{2,1,0:T(8,128)(2,1)}), bf16[64,8,1152]{2,1,0:T(8,128)(2,1)S(1)}, u32[]{:S(2)}, u32[]{:S(2)}) async-start(bf16[64,8,1152]{2,1,0:T(8,128)(2,1)} %bitcast.2), calls=%async_computation | async-start | bytes 2359296 | tf_op jit(solution)/shard_map/all_to_all | solution.py:201
  14.6 0.0 copy-start.7
  15.9 0.1 pad_maximum_fusion.scalars_ref
  16.0 0.0 copy-done
  16.0 2.3 %shard_map.77 = (f32[256,1152]{1,0:T(8,128)S(1)}, f32[256,1152]{1,0:T(8,128)S(1)}, f32[256,256]{1,0:T(8,128)S(1)}) custom-call(f32[2]{0:T(128)S(1)} %pad_maximum_fusion.scalars_ref, bf16[2,256,1152]{2,1,0:T(8,128)(2,1)S(1)} %copy-done), custom_call_target="tpu_custom_call" | custom-call | flops 603979776 | bytes 3538944 | tf_op jit(solution)/shard_map/pallas_call | solution.py:70
  18.3 0.0 copy-start.3
  18.3 1.0 %copy-done.3 = f32[256,1152]{1,0:T(8,128)} copy-done((f32[256,1152]{1,0:T(8,128)}, f32[256,1152]{1,0:T(8,128)S(1)}, u32[]{:S(2)}) %copy-start.3) | copy-done | bytes 1179672
  19.3 0.7 copy-done.5
  20.0 14.9 %all-to-all-done.same_ref = bf16[64,8,1152]{2,1,0:T(8,128)(2,1)S(1)} async-done(((bf16[64,8,1152]{2,1,0:T(8,128)(2,1)}), bf16[64,8,1152]{2,1,0:T(8,128)(2,1)S(1)}, u32[]{:S(2)}, u32[]{:S(2)}) %all-to-all-start) | async-done | bytes 1179680 | tf_op jit(solution)/shard_map/all_to_all | solution.py:201
  34.9 0.0 collective-permute-start
  34.9 0.0 copy-done.7
  34.9 0.1 slice_reduce_fusion.flips_ref
  35.0 2.7 %collective-permute-done.other_ref = bf16[64,8,1152]{2,1,0:T(8,128)(2,1)S(1)} collective-permute-done((bf16[64,8,1152]{2,1,0:T(8,128)(2,1)S(1)}, bf16[64,8,1152]{2,1,0:T(8,128)(2,1)S(1)}, u32[]{:S(2)}, u32[]{:S(2)}) %collective-permute-start) | collective-permute-done | bytes 1179680 | tf_op jit(solution)/shard_map/ppermute | solution.py:204
  37.7 0.9 %shard_map.78 = bf16[64,3,8,1152]{3,2,1,0:T(8,128)(2,1)S(1)} custom-call(s32[3]{0:T(128)S(1)} %slice_reduce_fusion.flips_ref, bf16[64,8,1152]{2,1,0:T(8,128)(2,1)S(1)} %all-to-all-done.same_ref, bf16[64,8,1152]{2,1,0:T(8,128)(2,1)S(1)} %collective-permute-done.other_ref), custom_call_target="tpu_custom_call" | custom-call | tf_op jit(solution)/shard_map/pallas_call | solution.py:107
  38.7 0.0 copy-start.1
  38.7 0.0 copy-start.2
  38.7 0.0 copy-start.4
  38.7 0.0 copy-start.6
  38.7 50.4 %all_to_all.10.far_ref = bf16[64,3,8,1152]{3,2,1,0:T(8,128)(2,1)S(1)} all-to-all(bf16[64,3,8,1152]{3,2,1,0:T(8,128)(2,1)S(1)} %shard_map.78), channel_id=1, replica_groups={{0,2,4,6,8,10,12,14,16,18,20,22,24,26,28,30,32,34,36,38,40,42,44,46,48,..., dimensions={0} | all-to-all | bytes 7077888 | tf_op jit(solution)/shard_map/all_to_all | solution.py:205
  89.1 0.0 copy-done.1
  89.1 0.0 copy-done.4
  89.1 0.0 copy-done.6
  89.1 4.9 %shard_map.79 = (f32[256,1152]{1,0:T(8,128)}, f32[256,1152]{1,0:T(8,128)}, f32[1,256]{1,0:T(1,128)}) custom-call(f32[2]{0:T(128)S(1)} %pad_maximum_fusion.scalars_ref, bf16[256,1152]{1,0:T(8,128)(2,1)S(1)} %copy-done.1, bf16[256,1152]{1,0:T(8,128)(2,1)S(1)} %copy-done.2, bf16[2,256,1152]{2,1,0:T(8,128)(2,1)S(1)} %copy-done, ...), custom_call_target="tpu_custom_call" | custom-call | tf_op jit(solution)/shard_map/pallas_call | solution.py:171
  (3 shorter events, 0.0 us)
Async XLA Ops:
  2.9 13.0 %copy-start = (bf16[2,256,1152]{2,1,0:T(8,128)(2,1)S(1)}, bf16[2,256,1152]{2,1,0:T(8,128)(2,1)}, u32[]{:S(2)}) copy-start(bf16[2,256,1152]{2,1,0:T(8,128)(2,1)} %shard_map.76.half_ref) | copy-start | bytes 3538948
  2.9 32.0 %all-to-all-start = ((bf16[64,8,1152]{2,1,0:T(8,128)(2,1)}), bf16[64,8,1152]{2,1,0:T(8,128)(2,1)S(1)}, u32[]{:S(2)}, u32[]{:S(2)}) async-start(bf16[64,8,1152]{2,1,0:T(8,128)(2,1)} %bitcast.2), calls=%async_computation | async-start | bytes 2359296 | tf_op jit(solution)/shard_map/all_to_all | solution.py:201
  14.6 20.3 %copy-start.7 = (s32[3,128]{1,0:T(4,128)S(1)}, s32[3,128]{1,0:T(4,128)}, u32[]{:S(2)}) copy-start(s32[3,128]{1,0:T(4,128)} %param.7) | copy-start | bytes 4612
  18.3 1.0 %copy-start.3 = (f32[256,1152]{1,0:T(8,128)}, f32[256,1152]{1,0:T(8,128)S(1)}, u32[]{:S(2)}) copy-start(f32[256,1152]{1,0:T(8,128)S(1)} %get-tuple-element.14.txt_sum_ref) | copy-start | bytes 3538948
  19.3 0.7 copy-start.5
  34.9 2.8 %collective-permute-start = (bf16[64,8,1152]{2,1,0:T(8,128)(2,1)S(1)}, bf16[64,8,1152]{2,1,0:T(8,128)(2,1)S(1)}, u32[]{:S(2)}, u32[]{:S(2)}) collective-permute-start(bf16[64,8,1152]{2,1,0:T(8,128)(2,1)S(1)} %all-to-all-done.same_ref), channel_id=1, source_target_pairs={{0,1},{1,0},{2,3},{3,2},{4,5},{5,4},{6,7},{7,6},{8,9},{9,8},{10,11... | collective-permute-start | bytes 3538952 | tf_op jit(solution)/shard_map/ppermute | solution.py:204
  38.7 50.4 %copy-start.1 = (bf16[256,1152]{1,0:T(8,128)(2,1)S(1)}, bf16[256,1152]{1,0:T(8,128)(2,1)}, u32[]{:S(2)}) copy-start(bf16[256,1152]{1,0:T(8,128)(2,1)} %images_ref.3) | copy-start | bytes 1769476
  38.7 50.4 %copy-start.2 = (bf16[256,1152]{1,0:T(8,128)(2,1)S(1)}, bf16[256,1152]{1,0:T(8,128)(2,1)}, u32[]{:S(2)}) copy-start(bf16[256,1152]{1,0:T(8,128)(2,1)} %texts_ref.3) | copy-start | bytes 1769476
  38.7 50.4 %copy-start.4 = (f32[256,1152]{1,0:T(8,128)S(1)}, f32[256,1152]{1,0:T(8,128)}, u32[]{:S(2)}) copy-start(f32[256,1152]{1,0:T(8,128)} %copy-done.3) | copy-start | bytes 3538948
  38.7 50.4 %copy-start.6 = (f32[256,256]{1,0:T(8,128)S(1)}, f32[256,256]{1,0:T(8,128)}, u32[]{:S(2)}) copy-start(f32[256,256]{1,0:T(8,128)} %copy-done.5) | copy-start | bytes 786436

commit v3 on v2

--- a/solution.py
+++ b/solution.py
@@ -12,7 +12,7 @@
 PIECE = 8
 CHUNKS = 2
 VMEM_BYTES = 20 * 1024 * 1024
-FULL_VMEM_BYTES = 61 * 1024 * 1024
+FULL_VMEM_BYTES = 60 * 1024 * 1024
 NT = (((1,), (1,)), ((), ()))
 
 
@@ -20,27 +20,33 @@
     return lax.rsqrt(jnp.sum(values * values, axis=-1, keepdims=True) + NORM_EPS)
 
 
-def halve_kernel(images_ref, texts_ref, half_ref):
-    for slot, source in enumerate((images_ref, texts_ref)):
-        values = source[...].astype(jnp.float32)
+def halve_kernel(images_ref, texts_ref, raw_ref, half_ref, sems):
+    copies = [
+        pltpu.make_async_copy(source, raw_ref.at[slot], sems.at[slot])
+        for slot, source in enumerate((images_ref, texts_ref))
+    ]
+    for copy in copies:
+        copy.start()
+    for slot, copy in enumerate(copies):
+        copy.wait()
+        values = raw_ref[slot].astype(jnp.float32)
         half_ref[slot] = (values * inverse_length(values)).astype(jnp.bfloat16)
 
 
 def halve(images, texts):
     rows, width = images.shape
-    step = rows // 2
     return pl.pallas_call(
         halve_kernel,
-        grid=(rows // step,),
-        in_specs=[pl.BlockSpec((step, width), lambda i: (i, 0))] * 2,
-        out_specs=pl.BlockSpec((2, step, width), lambda i: (0, i, 0)),
-        out_shape=jax.ShapeDtypeStruct((2, rows, width), jnp.bfloat16),
+        in_specs=[pl.BlockSpec(memory_space=pltpu.HBM)] * 2,
+        out_specs=[pl.BlockSpec(memory_space=pltpu.VMEM)] * 2,
+        out_shape=[pltpu.VMEM((2, rows, width), jnp.bfloat16)] * 2,
+        scratch_shapes=[pltpu.SemaphoreType.DMA((2,))],
         compiler_params=pltpu.CompilerParams(vmem_limit_bytes=FULL_VMEM_BYTES),
     )(images, texts)
 
 
-def own_kernel(scalars_ref, half_ref, img_sum_ref, txt_sum_ref, loss_ref):
-    scale, bias = scalars_ref[0], scalars_ref[1]
+def own_kernel(scale_ref, bias_ref, half_ref, img_sum_ref, txt_sum_ref, loss_ref):
+    scale, bias = scale_ref[0], bias_ref[0]
     img, txt = half_ref[0], half_ref[1]
     rows = img.shape[0]
     diagonal = lax.broadcasted_iota(jnp.int32, (rows, rows), 0) == lax.broadcasted_iota(
@@ -65,14 +71,11 @@
     return 1.0 / (1.0 + jnp.exp(-x))
 
 
-def own_terms(scalars, half):
+def own_terms(scale, bias, half):
     _, rows, width = half.shape
     return pl.pallas_call(
         own_kernel,
-        in_specs=[
-            pl.BlockSpec(memory_space=pltpu.SMEM),
-            pl.BlockSpec(memory_space=pltpu.VMEM),
-        ],
+        in_specs=[pl.BlockSpec(memory_space=pltpu.SMEM)] * 2 + [pl.BlockSpec(memory_space=pltpu.VMEM)],
         out_specs=[pl.BlockSpec(memory_space=pltpu.VMEM)] * 3,
         out_shape=[
             jax.ShapeDtypeStruct((rows, width), jnp.float32),
@@ -83,14 +86,14 @@
         cost_estimate=pl.CostEstimate(
             flops=8 * rows * rows * width, bytes_accessed=12 * rows * width, transcendentals=4 * rows * rows
         ),
-    )(scalars, half)
-
-
-def route_kernel(flips_ref, same_ref, other_ref, out_ref):
+    )(scale, bias, half)
+
+
+def route_kernel(partner_ref, same_ref, other_ref, out_ref):
     chips = same_ref.shape[0]
     for r in range(ROUNDS):
-        chip_flip = flips_ref[r] // 2
-        core_flip = flips_ref[r] % 2
+        chip_flip = partner_ref[r, 0] // 2
+        core_flip = partner_ref[r, 0] % 2
         for core, source in enumerate((same_ref, other_ref)):
 
             @pl.when(core_flip == core)
@@ -102,7 +105,7 @@
                 lax.fori_loop(0, chips, copy, 0, unroll=8)
 
 
-def route(flips, same, other):
+def route(partner, same, other):
     chips, piece, width = same.shape
     return pl.pallas_call(
         route_kernel,
@@ -111,7 +114,7 @@
         out_specs=pl.BlockSpec(memory_space=pltpu.VMEM),
         out_shape=jax.ShapeDtypeStruct((chips, ROUNDS, piece, width), same.dtype),
         compiler_params=pltpu.CompilerParams(vmem_limit_bytes=VMEM_BYTES),
-    )(flips, same, other)
+    )(partner, same, other)
 
 
 def finish(values, summed):
@@ -122,21 +125,21 @@
 
 
 def rounds_kernel(
-    scalars_ref, images_ref, texts_ref, half_ref, far_ref, img_sum_ref, txt_sum_ref, own_loss_ref,
+    scale_ref, bias_ref, raw_ref, half_ref, far_ref, img_sum_ref, txt_sum_ref, own_loss_ref,
     image_grad_ref, text_grad_ref, loss_ref, grads, loss, sems, loss_sem,
 ):
-    scale, bias = scalars_ref[0], scalars_ref[1]
+    scale, bias = scale_ref[0], bias_ref[0]
     img, txt = half_ref[0], half_ref[1]
     rows, width = img.shape
     pieces = far_ref.shape[0] // 2
     step = rows // CHUNKS
     copies = []
 
-    def send(slot, source, summed, out_ref):
+    def send(slot, summed, out_ref):
         for chunk in range(CHUNKS):
             part = pl.ds(chunk * step, step)
             grads[slot, part] = finish(
-                source[part].astype(jnp.float32), summed[chunk * step : (chunk + 1) * step]
+                raw_ref[slot, part].astype(jnp.float32), summed[chunk * step : (chunk + 1) * step]
             )
             copy = pltpu.make_async_copy(grads.at[slot, part], out_ref.at[part], sems.at[slot, chunk])
             copy.start()
@@ -146,7 +149,7 @@
     logits = scale * lax.dot_general(img, far_txt, NT, preferred_element_type=jnp.float32) + bias
     weights = sigmoid(logits).astype(jnp.bfloat16)
     summed = img_sum_ref[...] + scale * jnp.dot(weights, far_txt, preferred_element_type=jnp.float32)
-    send(0, images_ref, summed, image_grad_ref)
+    send(0, summed, image_grad_ref)
     parts = softplus(logits)
     losses = own_loss_ref[...]
     for r in range(ROUNDS):
@@ -161,17 +164,17 @@
         weights = sigmoid(logits).astype(jnp.bfloat16)
         term = scale * jnp.dot(weights, far_img, preferred_element_type=jnp.float32)
         summed = summed + term.astype(jnp.bfloat16).astype(jnp.float32)
-    send(1, texts_ref, summed, text_grad_ref)
+    send(1, summed, text_grad_ref)
     for copy in copies:
         copy.wait()
 
 
-def all_rounds(scalars, images, texts, half, far, img_sum, txt_sum, losses):
-    rows, width = images.shape
+def all_rounds(scale, bias, raw, half, far, img_sum, txt_sum, losses):
+    _, rows, width = raw.shape
     return pl.pallas_call(
         rounds_kernel,
-        in_specs=[pl.BlockSpec(memory_space=pltpu.SMEM)]
-        + [pl.BlockSpec(memory_space=pltpu.VMEM)] * 7,
+        in_specs=[pl.BlockSpec(memory_space=pltpu.SMEM)] * 2
+        + [pl.BlockSpec(memory_space=pltpu.VMEM)] * 6,
         out_specs=[pl.BlockSpec(memory_space=pltpu.HBM)] * 3,
         out_shape=[
             jax.ShapeDtypeStruct((rows, width), jnp.float32),
@@ -185,7 +188,7 @@
             pltpu.SemaphoreType.DMA,
         ],
         compiler_params=pltpu.CompilerParams(vmem_limit_bytes=VMEM_BYTES),
-    )(scalars, images, texts, half, far, img_sum, txt_sum, losses)
+    )(scale, bias, raw, half, far, img_sum, txt_sum, losses)
 
 
 def body(num_dev, images, texts, partner, logit_scale, logit_bias):
@@ -195,16 +198,15 @@
     exchange = functools.partial(
         lax.all_to_all, axis_name="dp", split_axis=0, concat_axis=0, tiled=True, axis_index_groups=same_core
     )
-    scalars = jnp.concatenate([logit_scale, logit_bias])
-    flips = partner[:, 0]
-    half = halve(images, texts)
+    raw, half = halve(images, texts)
     spread = exchange(half.reshape(chips, PIECE, width))
-    img_sum, txt_sum, losses = own_terms(scalars, half)
-    spread, img_sum = lax.optimization_barrier((spread, img_sum))
+    half, spread = lax.optimization_barrier((half, spread))
     sibling = lax.ppermute(spread, "dp", [(i, i ^ 1) for i in range(num_dev)])
-    far = exchange(route(flips, spread, sibling))
+    img_sum, txt_sum, losses = own_terms(logit_scale, logit_bias, half)
+    sibling, img_sum = lax.optimization_barrier((sibling, img_sum))
+    far = exchange(route(partner, spread, sibling))
     image_grad, text_grad, loss = all_rounds(
-        scalars, images, texts, half, far, img_sum, txt_sum, losses
+        logit_scale, logit_bias, raw, half, far, img_sum, txt_sum, losses
     )
     return image_grad, text_grad, loss.reshape(rows)
 

time: 94.4 us -> 93.3 us (0.988)
  blocking collectives: 50.4 us -> 82.4 us
  waiting for transfers between devices: 17.6 us -> 0.01 us
  starting transfers between devices: 11.6 us -> 0.01 us
  local copies, waits for them, and re-layouts: 1.87 us -> 0.01 us
  Pallas kernels: 10.5 us -> 8.74 us
    all_to_all x1 -> x2, blocking collectives: 50.4 us -> 82.4 us  [the longest x1 50.7 us: body(): far = exchange(route(partner, spread, sibling))]
    all_to_all x1 -> x0, waiting for transfers between devices: 14.9 us -> none  [body(): spread = exchange(half.reshape(chips, PIECE, width))]
    all_to_all x1 -> x0, starting transfers between devices: 11.6 us -> none  [body(): spread = exchange(half.reshape(chips, PIECE, width))]
    ppermute x1, waiting for transfers between devices: 2.73 us -> 0.01 us  [body(): sibling = lax.ppermute(spread, 'dp', [(i, i ^ 1) for i in range(num_dev)])]
    unnamed x16 -> x2, local copies, waits for them, and re-layouts: 1.75 us -> 0.01 us
  transfers between devices with their start and end apart: 2 -> 1, of which waited for: 2 -> 0; matrix products, arithmetic and copies ran while one was open for 0% -> 0% of each run, Pallas kernels for 2% -> 2%
where the time goes in v3:
time: 93.3 us; the launch traced here: 93.1 us
  blocking collectives  82.4 us (88%)
  Pallas kernels  8.74 us (9%)
  between operations  1.98 us (2%)
    all_to_all x1, blocking collectives, body(): far = exchange(route(partner, spread, sibling))  50.7 us
    all_to_all x1, blocking collectives, body(): spread = exchange(half.reshape(chips, PIECE, width))  31.6 us
    pallas_call x1, Pallas kernels, all_rounds(): pl.pallas_call(rounds_kernel, in_specs=[pl.BlockSpec(memory_space=pltpu.S...  4.48 us
  transfers between devices with their start and end apart: 1, of which 0 were waited for; matrix products, arithmetic and copies ran while one was open for 0% of the time, Pallas kernels for 2%

profile of v3, /device:TPU:0, one launch (start us, length us, event | category | flops | bytes accessed | tf_op | source)
XLA Modules:
  0.0 93.1 jit_solution(11787373439344890839)
XLA Ops:
  0.6 1.5 %shard_map.76 = (bf16[2,256,1152]{2,1,0:T(8,128)(2,1)S(1)}, bf16[2,256,1152]{2,1,0:T(8,128)(2,1)S(1)}) custom-call(bf16[256,1152]{1,0:T(8,128)(2,1)} %images_ref.1, bf16[256,1152]{1,0:T(8,128)(2,1)} %texts_ref.1), custom_call_target="tpu_custom_call" | custom-call | tf_op jit(solution)/shard_map/pallas_call | solution.py:38
  2.1 31.6 %all_to_all.10.same_ref = bf16[64,8,1152]{2,1,0:T(8,128)(2,1)S(1)} all-to-all(bf16[64,8,1152]{2,1,0:T(8,128)(2,1)S(1)} %bitcast.2), channel_id=1, replica_groups={{0,2,4,6,8,10,12,14,16,18,20,22,24,26,28,30,32,34,36,38,40,42,44,46,48,..., dimensions={0} | all-to-all | bytes 2359296 | tf_op jit(solution)/shard_map/all_to_all | solution.py:202
  33.7 0.0 copy-start
  33.7 0.0 collective-permute-start
  35.1 1.8 %shard_map.77 = (f32[256,1152]{1,0:T(8,128)S(1)}, f32[256,1152]{1,0:T(8,128)S(1)}, f32[256,256]{1,0:T(8,128)S(1)}) custom-call(f32[1]{0:T(128)S(6)} %copy.8.scale_ref, f32[1]{0:T(128)S(6)} %copy.9.bias_ref, bf16[2,256,1152]{2,1,0:T(8,128)(2,1)S(1)} %get-tuple-element.17.half_ref), custom_call_target="tpu_custom_call" | custom-call | flops 603979776 | bytes 3538944 | tf_op jit(solution)/shard_map/pallas_call | solution.py:76
  36.9 0.0 collective-permute-done.other_ref
  36.9 0.0 copy-done
  36.9 1.0 %shard_map.78 = bf16[64,3,8,1152]{3,2,1,0:T(8,128)(2,1)S(1)} custom-call(s32[3,128]{1,0:T(4,128)S(1)} %copy-done, bf16[64,8,1152]{2,1,0:T(8,128)(2,1)S(1)} %all_to_all.10.same_ref, bf16[64,8,1152]{2,1,0:T(8,128)(2,1)S(1)} %collective-permute-done.other_ref), custom_call_target="tpu_custom_call" | custom-call | tf_op jit(solution)/shard_map/pallas_call | solution.py:110
  37.9 50.7 %all_to_all.11.far_ref = bf16[64,3,8,1152]{3,2,1,0:T(8,128)(2,1)S(1)} all-to-all(bf16[64,3,8,1152]{3,2,1,0:T(8,128)(2,1)S(1)} %shard_map.78), channel_id=1, replica_groups={{0,2,4,6,8,10,12,14,16,18,20,22,24,26,28,30,32,34,36,38,40,42,44,46,48,..., dimensions={0} | all-to-all | bytes 7077888 | tf_op jit(solution)/shard_map/all_to_all | solution.py:207
  88.6 4.5 %shard_map.79 = (f32[256,1152]{1,0:T(8,128)}, f32[256,1152]{1,0:T(8,128)}, f32[1,256]{1,0:T(1,128)}) custom-call(f32[1]{0:T(128)S(6)} %copy.8.scale_ref, f32[1]{0:T(128)S(6)} %copy.9.bias_ref, bf16[2,256,1152]{2,1,0:T(8,128)(2,1)S(1)} %get-tuple-element.15.raw_ref, bf16[2,256,1152]{2,1,0:T(8,128)(2,1)S(1)} %get-tuple-element.17.half_ref, ...), custom_call_target="tpu_custom_call" | custom-call | tf_op jit(solution)/shard_map/pallas_call | solution.py:174
Async XLA Ops:
  33.7 3.1 %copy-start = (s32[3,128]{1,0:T(4,128)S(1)}, s32[3,128]{1,0:T(4,128)}, u32[]{:S(2)}) copy-start(s32[3,128]{1,0:T(4,128)} %partner_ref.1) | copy-start | bytes 4612
  33.7 3.1 %collective-permute-start = (bf16[64,8,1152]{2,1,0:T(8,128)(2,1)S(1)}, bf16[64,8,1152]{2,1,0:T(8,128)(2,1)S(1)}, u32[]{:S(2)}, u32[]{:S(2)}) collective-permute-start(bf16[64,8,1152]{2,1,0:T(8,128)(2,1)S(1)} %all_to_all.10.same_ref), channel_id=1, source_target_pairs={{0,1},{1,0},{2,3},{3,2},{4,5},{5,4},{6,7},{7,6},{8,9},{9,8},{10,11... | collective-permute-start | bytes 3538952 | tf_op jit(solution)/shard_map/ppermute | solution.py:204

commit v4 on v3

--- a/solution.py
+++ b/solution.py
@@ -10,17 +10,19 @@
 ROUNDS = 3
 NORM_EPS = 1e-06
 PIECE = 8
+CHIP_STEPS = (16, 32, 4, 8, 1, 2)
 CHUNKS = 2
 VMEM_BYTES = 20 * 1024 * 1024
 FULL_VMEM_BYTES = 60 * 1024 * 1024
 NT = (((1,), (1,)), ((), ()))
+TN = (((0,), (0,)), ((), ()))
 
 
 def inverse_length(values):
     return lax.rsqrt(jnp.sum(values * values, axis=-1, keepdims=True) + NORM_EPS)
 
 
-def halve_kernel(images_ref, texts_ref, raw_ref, half_ref, sems):
+def halve_kernel(images_ref, texts_ref, raw_ref, half_ref, inverse_ref, sems):
     copies = [
         pltpu.make_async_copy(source, raw_ref.at[slot], sems.at[slot])
         for slot, source in enumerate((images_ref, texts_ref))
@@ -30,7 +32,9 @@
     for slot, copy in enumerate(copies):
         copy.wait()
         values = raw_ref[slot].astype(jnp.float32)
-        half_ref[slot] = (values * inverse_length(values)).astype(jnp.bfloat16)
+        inverse = inverse_length(values)
+        inverse_ref[slot] = inverse
+        half_ref[slot] = (values * inverse).astype(jnp.bfloat16)
 
 
 def halve(images, texts):
@@ -38,8 +42,8 @@
     return pl.pallas_call(
         halve_kernel,
         in_specs=[pl.BlockSpec(memory_space=pltpu.HBM)] * 2,
-        out_specs=[pl.BlockSpec(memory_space=pltpu.VMEM)] * 2,
-        out_shape=[pltpu.VMEM((2, rows, width), jnp.bfloat16)] * 2,
+        out_specs=[pl.BlockSpec(memory_space=pltpu.VMEM)] * 3,
+        out_shape=[pltpu.VMEM((2, rows, width), jnp.bfloat16)] * 2 + [pltpu.VMEM((2, rows, 1), jnp.float32)],
         scratch_shapes=[pltpu.SemaphoreType.DMA((2,))],
         compiler_params=pltpu.CompilerParams(vmem_limit_bytes=FULL_VMEM_BYTES),
     )(images, texts)
@@ -58,9 +62,7 @@
     positive = jnp.where(diagonal, 1.0, 0.0)
     weights = (sigmoid(logits) - positive).astype(jnp.bfloat16)
     img_sum_ref[...] = scale * jnp.dot(weights, txt, preferred_element_type=jnp.float32)
-    turned = scale * lax.dot_general(txt, img, NT, preferred_element_type=jnp.float32) + bias
-    weights = (sigmoid(turned) - positive).astype(jnp.bfloat16)
-    txt_sum_ref[...] = scale * jnp.dot(weights, img, preferred_element_type=jnp.float32)
+    txt_sum_ref[...] = scale * lax.dot_general(weights, img, TN, preferred_element_type=jnp.float32)
 
 
 def softplus(x):
@@ -89,10 +91,24 @@
     )(scale, bias, half)
 
 
+def slot_chip(slot):
+    chip = 0
+    for bit, step in enumerate(CHIP_STEPS):
+        chip ^= step * ((slot >> bit) & 1)
+    return chip
+
+
+def chip_slot(chip):
+    slot = 0
+    for bit, step in enumerate(CHIP_STEPS):
+        slot += (chip // step % 2) << bit
+    return slot
+
+
 def route_kernel(partner_ref, same_ref, other_ref, out_ref):
     chips = same_ref.shape[0]
     for r in range(ROUNDS):
-        chip_flip = partner_ref[r, 0] // 2
+        chip_flip = chip_slot(partner_ref[r, 0] // 2)
         core_flip = partner_ref[r, 0] % 2
         for core, source in enumerate((same_ref, other_ref)):
 
@@ -117,15 +133,14 @@
     )(partner, same, other)
 
 
-def finish(values, summed):
-    inverse = inverse_length(values)
+def finish(values, inverse, summed):
     unit = values * inverse
     radial = jnp.sum(unit * summed, axis=-1, keepdims=True)
     return (summed - unit * radial) * inverse
 
 
 def rounds_kernel(
-    scale_ref, bias_ref, raw_ref, half_ref, far_ref, img_sum_ref, txt_sum_ref, own_loss_ref,
+    scale_ref, bias_ref, raw_ref, half_ref, inverse_ref, far_ref, img_sum_ref, txt_sum_ref, own_loss_ref,
     image_grad_ref, text_grad_ref, loss_ref, grads, loss, sems, loss_sem,
 ):
     scale, bias = scale_ref[0], bias_ref[0]
@@ -139,7 +154,9 @@
         for chunk in range(CHUNKS):
             part = pl.ds(chunk * step, step)
             grads[slot, part] = finish(
-                raw_ref[slot, part].astype(jnp.float32), summed[chunk * step : (chunk + 1) * step]
+                raw_ref[slot, part].astype(jnp.float32),
+                inverse_ref[slot, part],
+                summed[chunk * step : (chunk + 1) * step],
             )
             copy = pltpu.make_async_copy(grads.at[slot, part], out_ref.at[part], sems.at[slot, chunk])
             copy.start()
@@ -158,10 +175,14 @@
     copies.append(pltpu.make_async_copy(loss, loss_ref, loss_sem))
     copies[-1].start()
     summed = txt_sum_ref[...]
+    turned = []
     for r in range(ROUNDS):
         far_img = far_ref[:pieces, r].reshape(rows, width)
         logits = scale * lax.dot_general(txt, far_img, NT, preferred_element_type=jnp.float32) + bias
-        weights = sigmoid(logits).astype(jnp.bfloat16)
+        turned.append(sigmoid(logits).astype(jnp.bfloat16))
+    for r in range(ROUNDS):
+        far_img = far_ref[:pieces, r].reshape(rows, width)
+        weights = turned[r]
         term = scale * jnp.dot(weights, far_img, preferred_element_type=jnp.float32)
         summed = summed + term.astype(jnp.bfloat16).astype(jnp.float32)
     send(1, summed, text_grad_ref)
@@ -169,12 +190,12 @@
         copy.wait()
 
 
-def all_rounds(scale, bias, raw, half, far, img_sum, txt_sum, losses):
+def all_rounds(scale, bias, raw, half, inverse, far, img_sum, txt_sum, losses):
     _, rows, width = raw.shape
     return pl.pallas_call(
         rounds_kernel,
         in_specs=[pl.BlockSpec(memory_space=pltpu.SMEM)] * 2
-        + [pl.BlockSpec(memory_space=pltpu.VMEM)] * 6,
+        + [pl.BlockSpec(memory_space=pltpu.VMEM)] * 7,
         out_specs=[pl.BlockSpec(memory_space=pltpu.HBM)] * 3,
         out_shape=[
             jax.ShapeDtypeStruct((rows, width), jnp.float32),
@@ -188,17 +209,17 @@
             pltpu.SemaphoreType.DMA,
         ],
         compiler_params=pltpu.CompilerParams(vmem_limit_bytes=VMEM_BYTES),
-    )(scale, bias, raw, half, far, img_sum, txt_sum, losses)
+    )(scale, bias, raw, half, inverse, far, img_sum, txt_sum, losses)
 
 
 def body(num_dev, images, texts, partner, logit_scale, logit_bias):
     rows, width = images.shape
     chips = num_dev // 2
-    same_core = [[2 * chip + core for chip in range(chips)] for core in range(2)]
+    same_core = [[2 * slot_chip(slot) + core for slot in range(chips)] for core in range(2)]
     exchange = functools.partial(
         lax.all_to_all, axis_name="dp", split_axis=0, concat_axis=0, tiled=True, axis_index_groups=same_core
     )
-    raw, half = halve(images, texts)
+    raw, half, inverse = halve(images, texts)
     spread = exchange(half.reshape(chips, PIECE, width))
     half, spread = lax.optimization_barrier((half, spread))
     sibling = lax.ppermute(spread, "dp", [(i, i ^ 1) for i in range(num_dev)])
@@ -206,7 +227,7 @@
     sibling, img_sum = lax.optimization_barrier((sibling, img_sum))
     far = exchange(route(partner, spread, sibling))
     image_grad, text_grad, loss = all_rounds(
-        logit_scale, logit_bias, raw, half, far, img_sum, txt_sum, losses
+        logit_scale, logit_bias, raw, half, inverse, far, img_sum, txt_sum, losses
     )
     return image_grad, text_grad, loss.reshape(rows)
 

time: 93.3 us -> 92.1 us (0.987)
  transfers between devices with their start and end apart: 1 -> 1, of which waited for: 0 -> 1; matrix products, arithmetic and copies ran while one was open for 0% -> 0% of each run, Pallas kernels for 2% -> 1%
where the time goes in v4:
time: 92.1 us; the launch traced here: 91.8 us
  blocking collectives  81.6 us (89%)
  Pallas kernels  8 us (9%)
  between operations  1.96 us (2%)
    all_to_all x1, blocking collectives, body(): far = exchange(route(partner, spread, sibling))  50.2 us
    all_to_all x1, blocking collectives, body(): spread = exchange(half.reshape(chips, PIECE, width))  31.4 us
    pallas_call x1, Pallas kernels, all_rounds(): pl.pallas_call(rounds_kernel, in_specs=[pl.BlockSpec(memory_space=pltpu.S...  4.21 us
  transfers between devices with their start and end apart: 1, of which 1 were waited for; matrix products, arithmetic and copies ran while one was open for 0% of the time, Pallas kernels for 1%

profile of v4, /device:TPU:0, one launch (start us, length us, event | category | flops | bytes accessed | tf_op | source)
XLA Modules:
  0.0 91.8 jit_solution(3734439656340156418)
XLA Ops:
  0.6 1.5 %shard_map.76 = (bf16[2,256,1152]{2,1,0:T(8,128)(2,1)S(1)}, bf16[2,256,1152]{2,1,0:T(8,128)(2,1)S(1)}, f32[2,256,1]{2,1,0:T(8,128)S(1)}) custom-call(bf16[256,1152]{1,0:T(8,128)(2,1)} %images_ref.1, bf16[256,1152]{1,0:T(8,128)(2,1)} %texts_ref.1), custom_call_target="tpu_custom_call" | custom-call | tf_op jit(solution)/shard_map/pallas_call | solution.py:42
  2.1 31.4 %all_to_all.10.same_ref = bf16[64,8,1152]{2,1,0:T(8,128)(2,1)S(1)} all-to-all(bf16[64,8,1152]{2,1,0:T(8,128)(2,1)S(1)} %bitcast.2), channel_id=1, replica_groups={{0,32,64,96,8,40,72,104,16,48,80,112,24,56,88,120,2,34,66,98,10,42,74,1..., dimensions={0} | all-to-all | bytes 2359296 | tf_op jit(solution)/shard_map/all_to_all | solution.py:223
  33.5 0.0 copy-start
  33.5 0.0 collective-permute-start
  34.8 1.3 %shard_map.77 = (f32[256,1152]{1,0:T(8,128)S(1)}, f32[256,1152]{1,0:T(8,128)S(1)}, f32[256,256]{1,0:T(8,128)S(1)}) custom-call(f32[1]{0:T(128)S(6)} %copy.8.scale_ref, f32[1]{0:T(128)S(6)} %copy.9.bias_ref, bf16[2,256,1152]{2,1,0:T(8,128)(2,1)S(1)} %get-tuple-element.18.half_ref), custom_call_target="tpu_custom_call" | custom-call | flops 603979776 | bytes 3538944 | tf_op jit(solution)/shard_map/pallas_call | solution.py:78
  36.1 0.3 collective-permute-done.other_ref
  36.4 0.0 copy-done
  36.4 1.1 %shard_map.78 = bf16[64,3,8,1152]{3,2,1,0:T(8,128)(2,1)S(1)} custom-call(s32[3,128]{1,0:T(4,128)S(1)} %copy-done, bf16[64,8,1152]{2,1,0:T(8,128)(2,1)S(1)} %all_to_all.10.same_ref, bf16[64,8,1152]{2,1,0:T(8,128)(2,1)S(1)} %collective-permute-done.other_ref), custom_call_target="tpu_custom_call" | custom-call | tf_op jit(solution)/shard_map/pallas_call | solution.py:126
  37.4 50.2 %all_to_all.11.far_ref = bf16[64,3,8,1152]{3,2,1,0:T(8,128)(2,1)S(1)} all-to-all(bf16[64,3,8,1152]{3,2,1,0:T(8,128)(2,1)S(1)} %shard_map.78), channel_id=1, replica_groups={{0,32,64,96,8,40,72,104,16,48,80,112,24,56,88,120,2,34,66,98,10,42,74,1..., dimensions={0} | all-to-all | bytes 7077888 | tf_op jit(solution)/shard_map/all_to_all | solution.py:228
  87.6 4.2 %shard_map.79 = (f32[256,1152]{1,0:T(8,128)}, f32[256,1152]{1,0:T(8,128)}, f32[1,256]{1,0:T(1,128)}) custom-call(f32[1]{0:T(128)S(6)} %copy.8.scale_ref, f32[1]{0:T(128)S(6)} %copy.9.bias_ref, bf16[2,256,1152]{2,1,0:T(8,128)(2,1)S(1)} %get-tuple-element.16.raw_ref, bf16[2,256,1152]{2,1,0:T(8,128)(2,1)S(1)} %get-tuple-element.18.half_ref, ...), custom_call_target="tpu_custom_call" | custom-call | tf_op jit(solution)/shard_map/pallas_call | solution.py:195
Async XLA Ops:
  33.5 2.9 %copy-start = (s32[3,128]{1,0:T(4,128)S(1)}, s32[3,128]{1,0:T(4,128)}, u32[]{:S(2)}) copy-start(s32[3,128]{1,0:T(4,128)} %partner_ref.1) | copy-start | bytes 4612
  33.5 2.8 %collective-permute-start = (bf16[64,8,1152]{2,1,0:T(8,128)(2,1)S(1)}, bf16[64,8,1152]{2,1,0:T(8,128)(2,1)S(1)}, u32[]{:S(2)}, u32[]{:S(2)}) collective-permute-start(bf16[64,8,1152]{2,1,0:T(8,128)(2,1)S(1)} %all_to_all.10.same_ref), channel_id=1, source_target_pairs={{0,1},{1,0},{2,3},{3,2},{4,5},{5,4},{6,7},{7,6},{8,9},{9,8},{10,11... | collective-permute-start | bytes 3538952 | tf_op jit(solution)/shard_map/ppermute | solution.py:225

commit v5 on v4

--- a/solution.py
+++ b/solution.py
@@ -10,7 +10,7 @@
 ROUNDS = 3
 NORM_EPS = 1e-06
 PIECE = 8
-CHIP_STEPS = (16, 32, 4, 8, 1, 2)
+CHIP_STEPS = (16, 32, 8, 4, 1, 2)
 CHUNKS = 2
 VMEM_BYTES = 20 * 1024 * 1024
 FULL_VMEM_BYTES = 60 * 1024 * 1024
@@ -118,7 +118,7 @@
                     out_ref[t, r] = source[lax.bitwise_xor(t, chip_flip)]
                     return carry
 
-                lax.fori_loop(0, chips, copy, 0, unroll=8)
+                lax.fori_loop(0, chips, copy, 0, unroll=16)
 
 
 def route(partner, same, other):

time: 92.1 us -> 91.4 us (level)
  no operation moved by 1% of the time
where the time goes in v5:
time: 91.4 us; the launch traced here: 91.1 us
  blocking collectives  80.9 us (89%)
  Pallas kernels  7.95 us (9%)
  between operations  1.96 us (2%)
    all_to_all x1, blocking collectives, body(): far = exchange(route(partner, spread, sibling))  50 us
    all_to_all x1, blocking collectives, body(): spread = exchange(half.reshape(chips, PIECE, width))  30.9 us
    pallas_call x1, Pallas kernels, all_rounds(): pl.pallas_call(rounds_kernel, in_specs=[pl.BlockSpec(memory_space=pltpu.S...  4.21 us
  transfers between devices with their start and end apart: 1, of which 1 were waited for; matrix products, arithmetic and copies ran while one was open for 0% of the time, Pallas kernels for 1%

profile of v5, /device:TPU:0, one launch (start us, length us, event | category | flops | bytes accessed | tf_op | source)
XLA Modules:
  0.0 91.1 jit_solution(8387225770869583582)
XLA Ops:
  0.6 1.5 %shard_map.76 = (bf16[2,256,1152]{2,1,0:T(8,128)(2,1)S(1)}, bf16[2,256,1152]{2,1,0:T(8,128)(2,1)S(1)}, f32[2,256,1]{2,1,0:T(8,128)S(1)}) custom-call(bf16[256,1152]{1,0:T(8,128)(2,1)} %images_ref.1, bf16[256,1152]{1,0:T(8,128)(2,1)} %texts_ref.1), custom_call_target="tpu_custom_call" | custom-call | tf_op jit(solution)/shard_map/pallas_call | solution.py:42
  2.1 30.9 %all_to_all.10.same_ref = bf16[64,8,1152]{2,1,0:T(8,128)(2,1)S(1)} all-to-all(bf16[64,8,1152]{2,1,0:T(8,128)(2,1)S(1)} %bitcast.2), channel_id=1, replica_groups={{0,32,64,96,16,48,80,112,8,40,72,104,24,56,88,120,2,34,66,98,18,50,82,1..., dimensions={0} | all-to-all | bytes 2359296 | tf_op jit(solution)/shard_map/all_to_all | solution.py:223
  33.0 0.0 copy-start
  33.0 0.0 collective-permute-start
  34.3 1.3 %shard_map.77 = (f32[256,1152]{1,0:T(8,128)S(1)}, f32[256,1152]{1,0:T(8,128)S(1)}, f32[256,256]{1,0:T(8,128)S(1)}) custom-call(f32[1]{0:T(128)S(6)} %copy.8.scale_ref, f32[1]{0:T(128)S(6)} %copy.9.bias_ref, bf16[2,256,1152]{2,1,0:T(8,128)(2,1)S(1)} %get-tuple-element.18.half_ref), custom_call_target="tpu_custom_call" | custom-call | flops 603979776 | bytes 3538944 | tf_op jit(solution)/shard_map/pallas_call | solution.py:78
  35.6 0.3 collective-permute-done.other_ref
  35.9 0.0 copy-done
  35.9 1.0 %shard_map.78 = bf16[64,3,8,1152]{3,2,1,0:T(8,128)(2,1)S(1)} custom-call(s32[3,128]{1,0:T(4,128)S(1)} %copy-done, bf16[64,8,1152]{2,1,0:T(8,128)(2,1)S(1)} %all_to_all.10.same_ref, bf16[64,8,1152]{2,1,0:T(8,128)(2,1)S(1)} %collective-permute-done.other_ref), custom_call_target="tpu_custom_call" | custom-call | tf_op jit(solution)/shard_map/pallas_call | solution.py:126
  36.9 50.0 %all_to_all.11.far_ref = bf16[64,3,8,1152]{3,2,1,0:T(8,128)(2,1)S(1)} all-to-all(bf16[64,3,8,1152]{3,2,1,0:T(8,128)(2,1)S(1)} %shard_map.78), channel_id=1, replica_groups={{0,32,64,96,16,48,80,112,8,40,72,104,24,56,88,120,2,34,66,98,18,50,82,1..., dimensions={0} | all-to-all | bytes 7077888 | tf_op jit(solution)/shard_map/all_to_all | solution.py:228
  86.9 4.2 %shard_map.79 = (f32[256,1152]{1,0:T(8,128)}, f32[256,1152]{1,0:T(8,128)}, f32[1,256]{1,0:T(1,128)}) custom-call(f32[1]{0:T(128)S(6)} %copy.8.scale_ref, f32[1]{0:T(128)S(6)} %copy.9.bias_ref, bf16[2,256,1152]{2,1,0:T(8,128)(2,1)S(1)} %get-tuple-element.16.raw_ref, bf16[2,256,1152]{2,1,0:T(8,128)(2,1)S(1)} %get-tuple-element.18.half_ref, ...), custom_call_target="tpu_custom_call" | custom-call | tf_op jit(solution)/shard_map/pallas_call | solution.py:195
Async XLA Ops:
  33.0 2.9 %copy-start = (s32[3,128]{1,0:T(4,128)S(1)}, s32[3,128]{1,0:T(4,128)}, u32[]{:S(2)}) copy-start(s32[3,128]{1,0:T(4,128)} %partner_ref.1) | copy-start | bytes 4612
  33.0 2.8 %collective-permute-start = (bf16[64,8,1152]{2,1,0:T(8,128)(2,1)S(1)}, bf16[64,8,1152]{2,1,0:T(8,128)(2,1)S(1)}, u32[]{:S(2)}, u32[]{:S(2)}) collective-permute-start(bf16[64,8,1152]{2,1,0:T(8,128)(2,1)S(1)} %all_to_all.10.same_ref), channel_id=1, source_target_pairs={{0,1},{1,0},{2,3},{3,2},{4,5},{5,4},{6,7},{7,6},{8,9},{9,8},{10,11... | collective-permute-start | bytes 3538952 | tf_op jit(solution)/shard_map/ppermute | solution.py:225

commit v6 on v5

--- a/solution.py
+++ b/solution.py
@@ -9,6 +9,7 @@
 
 ROUNDS = 3
 NORM_EPS = 1e-06
+LOG2_E = 1.4426950408889634
 PIECE = 8
 CHIP_STEPS = (16, 32, 8, 4, 1, 2)
 CHUNKS = 2
@@ -175,11 +176,12 @@
     copies.append(pltpu.make_async_copy(loss, loss_ref, loss_sem))
     copies[-1].start()
     summed = txt_sum_ref[...]
+    steep, shift = -LOG2_E * scale, -LOG2_E * bias
     turned = []
     for r in range(ROUNDS):
         far_img = far_ref[:pieces, r].reshape(rows, width)
-        logits = scale * lax.dot_general(txt, far_img, NT, preferred_element_type=jnp.float32) + bias
-        turned.append(sigmoid(logits).astype(jnp.bfloat16))
+        product = lax.dot_general(txt, far_img, NT, preferred_element_type=jnp.float32)
+        turned.append((1.0 / (1.0 + jnp.exp2(steep * product + shift))).astype(jnp.bfloat16))
     for r in range(ROUNDS):
         far_img = far_ref[:pieces, r].reshape(rows, width)
         weights = turned[r]

time: 91.4 us -> 91.3 us (level)
  no operation moved by 1% of the time
where the time goes in v6:
time: 91.3 us; the launch traced here: 91.1 us
  blocking collectives  80.9 us (89%)
  Pallas kernels  7.94 us (9%)
  between operations  1.96 us (2%)
    all_to_all x1, blocking collectives, body(): far = exchange(route(partner, spread, sibling))  50 us
    all_to_all x1, blocking collectives, body(): spread = exchange(half.reshape(chips, PIECE, width))  30.9 us
    pallas_call x1, Pallas kernels, all_rounds(): pl.pallas_call(rounds_kernel, in_specs=[pl.BlockSpec(memory_space=pltpu.S...  4.19 us
  transfers between devices with their start and end apart: 1, of which 1 were waited for; matrix products, arithmetic and copies ran while one was open for 0% of the time, Pallas kernels for 1%

profile of v6, /device:TPU:0, one launch (start us, length us, event | category | flops | bytes accessed | tf_op | source)
XLA Modules:
  0.0 91.1 jit_solution(13869754637343997999)
XLA Ops:
  0.6 1.5 %shard_map.76 = (bf16[2,256,1152]{2,1,0:T(8,128)(2,1)S(1)}, bf16[2,256,1152]{2,1,0:T(8,128)(2,1)S(1)}, f32[2,256,1]{2,1,0:T(8,128)S(1)}) custom-call(bf16[256,1152]{1,0:T(8,128)(2,1)} %images_ref.1, bf16[256,1152]{1,0:T(8,128)(2,1)} %texts_ref.1), custom_call_target="tpu_custom_call" | custom-call | tf_op jit(solution)/shard_map/pallas_call | solution.py:43
  2.1 30.9 %all_to_all.10.same_ref = bf16[64,8,1152]{2,1,0:T(8,128)(2,1)S(1)} all-to-all(bf16[64,8,1152]{2,1,0:T(8,128)(2,1)S(1)} %bitcast.2), channel_id=1, replica_groups={{0,32,64,96,16,48,80,112,8,40,72,104,24,56,88,120,2,34,66,98,18,50,82,1..., dimensions={0} | all-to-all | bytes 2359296 | tf_op jit(solution)/shard_map/all_to_all | solution.py:225
  33.0 0.0 copy-start
  33.0 0.0 collective-permute-start
  34.3 1.3 %shard_map.77 = (f32[256,1152]{1,0:T(8,128)S(1)}, f32[256,1152]{1,0:T(8,128)S(1)}, f32[256,256]{1,0:T(8,128)S(1)}) custom-call(f32[1]{0:T(128)S(6)} %copy.8.scale_ref, f32[1]{0:T(128)S(6)} %copy.9.bias_ref, bf16[2,256,1152]{2,1,0:T(8,128)(2,1)S(1)} %get-tuple-element.18.half_ref), custom_call_target="tpu_custom_call" | custom-call | flops 603979776 | bytes 3538944 | tf_op jit(solution)/shard_map/pallas_call | solution.py:79
  35.6 0.3 collective-permute-done.other_ref
  35.9 0.0 copy-done
  35.9 1.0 %shard_map.78 = bf16[64,3,8,1152]{3,2,1,0:T(8,128)(2,1)S(1)} custom-call(s32[3,128]{1,0:T(4,128)S(1)} %copy-done, bf16[64,8,1152]{2,1,0:T(8,128)(2,1)S(1)} %all_to_all.10.same_ref, bf16[64,8,1152]{2,1,0:T(8,128)(2,1)S(1)} %collective-permute-done.other_ref), custom_call_target="tpu_custom_call" | custom-call | tf_op jit(solution)/shard_map/pallas_call | solution.py:127
  36.9 50.0 %all_to_all.11.far_ref = bf16[64,3,8,1152]{3,2,1,0:T(8,128)(2,1)S(1)} all-to-all(bf16[64,3,8,1152]{3,2,1,0:T(8,128)(2,1)S(1)} %shard_map.78), channel_id=1, replica_groups={{0,32,64,96,16,48,80,112,8,40,72,104,24,56,88,120,2,34,66,98,18,50,82,1..., dimensions={0} | all-to-all | bytes 7077888 | tf_op jit(solution)/shard_map/all_to_all | solution.py:230
  86.9 4.2 %shard_map.79 = (f32[256,1152]{1,0:T(8,128)}, f32[256,1152]{1,0:T(8,128)}, f32[1,256]{1,0:T(1,128)}) custom-call(f32[1]{0:T(128)S(6)} %copy.8.scale_ref, f32[1]{0:T(128)S(6)} %copy.9.bias_ref, bf16[2,256,1152]{2,1,0:T(8,128)(2,1)S(1)} %get-tuple-element.16.raw_ref, bf16[2,256,1152]{2,1,0:T(8,128)(2,1)S(1)} %get-tuple-element.18.half_ref, ...), custom_call_target="tpu_custom_call" | custom-call | tf_op jit(solution)/shard_map/pallas_call | solution.py:197
Async XLA Ops:
  33.0 2.9 %copy-start = (s32[3,128]{1,0:T(4,128)S(1)}, s32[3,128]{1,0:T(4,128)}, u32[]{:S(2)}) copy-start(s32[3,128]{1,0:T(4,128)} %partner_ref.1) | copy-start | bytes 4612
  33.0 2.8 %collective-permute-start = (bf16[64,8,1152]{2,1,0:T(8,128)(2,1)S(1)}, bf16[64,8,1152]{2,1,0:T(8,128)(2,1)S(1)}, u32[]{:S(2)}, u32[]{:S(2)}) collective-permute-start(bf16[64,8,1152]{2,1,0:T(8,128)(2,1)S(1)} %all_to_all.10.same_ref), channel_id=1, source_target_pairs={{0,1},{1,0},{2,3},{3,2},{4,5},{5,4},{6,7},{7,6},{8,9},{9,8},{10,11... | collective-permute-start | bytes 3538952 | tf_op jit(solution)/shard_map/ppermute | solution.py:227

commit v7 on v6

--- a/solution.py
+++ b/solution.py
@@ -119,7 +119,7 @@
                     out_ref[t, r] = source[lax.bitwise_xor(t, chip_flip)]
                     return carry
 
-                lax.fori_loop(0, chips, copy, 0, unroll=16)
+                lax.fori_loop(0, chips, copy, 0, unroll=32)
 
 
 def route(partner, same, other):

time: 91.3 us -> 91.3 us (level)
  no operation moved by 1% of the time
where the time goes in v7:
time: 91.3 us; the launch traced here: 91.1 us
  blocking collectives  80.9 us (89%)
  Pallas kernels  7.91 us (9%)
  between operations  1.96 us (2%)
    all_to_all x1, blocking collectives, body(): far = exchange(route(partner, spread, sibling))  50 us
    all_to_all x1, blocking collectives, body(): spread = exchange(half.reshape(chips, PIECE, width))  30.9 us
    pallas_call x1, Pallas kernels, all_rounds(): pl.pallas_call(rounds_kernel, in_specs=[pl.BlockSpec(memory_space=pltpu.S...  4.2 us
  transfers between devices with their start and end apart: 1, of which 1 were waited for; matrix products, arithmetic and copies ran while one was open for 0% of the time, Pallas kernels for 1%

profile of v7, /device:TPU:0, one launch (start us, length us, event | category | flops | bytes accessed | tf_op | source)
XLA Modules:
  0.0 91.1 jit_solution(1943592921054875250)
XLA Ops:
  0.6 1.5 %shard_map.76 = (bf16[2,256,1152]{2,1,0:T(8,128)(2,1)S(1)}, bf16[2,256,1152]{2,1,0:T(8,128)(2,1)S(1)}, f32[2,256,1]{2,1,0:T(8,128)S(1)}) custom-call(bf16[256,1152]{1,0:T(8,128)(2,1)} %images_ref.1, bf16[256,1152]{1,0:T(8,128)(2,1)} %texts_ref.1), custom_call_target="tpu_custom_call" | custom-call | tf_op jit(solution)/shard_map/pallas_call | solution.py:43
  2.1 30.9 %all_to_all.10.same_ref = bf16[64,8,1152]{2,1,0:T(8,128)(2,1)S(1)} all-to-all(bf16[64,8,1152]{2,1,0:T(8,128)(2,1)S(1)} %bitcast.2), channel_id=1, replica_groups={{0,32,64,96,16,48,80,112,8,40,72,104,24,56,88,120,2,34,66,98,18,50,82,1..., dimensions={0} | all-to-all | bytes 2359296 | tf_op jit(solution)/shard_map/all_to_all | solution.py:225
  33.0 0.0 copy-start
  33.0 0.0 collective-permute-start
  34.3 1.3 %shard_map.77 = (f32[256,1152]{1,0:T(8,128)S(1)}, f32[256,1152]{1,0:T(8,128)S(1)}, f32[256,256]{1,0:T(8,128)S(1)}) custom-call(f32[1]{0:T(128)S(6)} %copy.8.scale_ref, f32[1]{0:T(128)S(6)} %copy.9.bias_ref, bf16[2,256,1152]{2,1,0:T(8,128)(2,1)S(1)} %get-tuple-element.18.half_ref), custom_call_target="tpu_custom_call" | custom-call | flops 603979776 | bytes 3538944 | tf_op jit(solution)/shard_map/pallas_call | solution.py:79
  35.6 0.3 collective-permute-done.other_ref
  35.9 0.0 copy-done
  35.9 1.0 %shard_map.78 = bf16[64,3,8,1152]{3,2,1,0:T(8,128)(2,1)S(1)} custom-call(s32[3,128]{1,0:T(4,128)S(1)} %copy-done, bf16[64,8,1152]{2,1,0:T(8,128)(2,1)S(1)} %all_to_all.10.same_ref, bf16[64,8,1152]{2,1,0:T(8,128)(2,1)S(1)} %collective-permute-done.other_ref), custom_call_target="tpu_custom_call" | custom-call | tf_op jit(solution)/shard_map/pallas_call | solution.py:127
  36.9 50.0 %all_to_all.11.far_ref = bf16[64,3,8,1152]{3,2,1,0:T(8,128)(2,1)S(1)} all-to-all(bf16[64,3,8,1152]{3,2,1,0:T(8,128)(2,1)S(1)} %shard_map.78), channel_id=1, replica_groups={{0,32,64,96,16,48,80,112,8,40,72,104,24,56,88,120,2,34,66,98,18,50,82,1..., dimensions={0} | all-to-all | bytes 7077888 | tf_op jit(solution)/shard_map/all_to_all | solution.py:230
  86.9 4.2 %shard_map.79 = (f32[256,1152]{1,0:T(8,128)}, f32[256,1152]{1,0:T(8,128)}, f32[1,256]{1,0:T(1,128)}) custom-call(f32[1]{0:T(128)S(6)} %copy.8.scale_ref, f32[1]{0:T(128)S(6)} %copy.9.bias_ref, bf16[2,256,1152]{2,1,0:T(8,128)(2,1)S(1)} %get-tuple-element.16.raw_ref, bf16[2,256,1152]{2,1,0:T(8,128)(2,1)S(1)} %get-tuple-element.18.half_ref, ...), custom_call_target="tpu_custom_call" | custom-call | tf_op jit(solution)/shard_map/pallas_call | solution.py:197
Async XLA Ops:
  33.0 2.9 %copy-start = (s32[3,128]{1,0:T(4,128)S(1)}, s32[3,128]{1,0:T(4,128)}, u32[]{:S(2)}) copy-start(s32[3,128]{1,0:T(4,128)} %partner_ref.1) | copy-start | bytes 4612
  33.0 2.8 %collective-permute-start = (bf16[64,8,1152]{2,1,0:T(8,128)(2,1)S(1)}, bf16[64,8,1152]{2,1,0:T(8,128)(2,1)S(1)}, u32[]{:S(2)}, u32[]{:S(2)}) collective-permute-start(bf16[64,8,1152]{2,1,0:T(8,128)(2,1)S(1)} %all_to_all.10.same_ref), channel_id=1, source_target_pairs={{0,1},{1,0},{2,3},{3,2},{4,5},{5,4},{6,7},{7,6},{8,9},{9,8},{10,11... | collective-permute-start | bytes 3538952 | tf_op jit(solution)/shard_map/ppermute | solution.py:227
